TPU v7x, 512 devices: a whole 4x4x16 slice. The times are simulated.
512 devices in a mesh: blk: 32 (over z, y_lo), head: 16 (over y_hi, x, core).
Axes of the slice: x: 4, y: 4 (y_hi: 2, y_lo: 2; y = y_hi * 2 + y_lo), z: 16, core: 2. Of those that a mesh axis runs over, the one named last changes fastest.
Arguments:
- node_feats: bfloat16 [65536, 512], P(('blk', 'head')), may hold values from -16 to 16
- graph_ids: int32 [65536], replicated, may hold values from 0 to 4095, never falling along the last dimension, each value on 1 to 32 neighbouring positions
- pair_tiles: int32 [32, 32, 8], P('blk'), may hold values from 0 to 255, as said below
- pair_count: int32 [32, 32], P('blk'), may hold values from 0 to 8, as said below
- w_query: bfloat16 [512, 512], replicated, may hold values from -0.4375 to 0.4375
- w_key: bfloat16 [512, 512], replicated, may hold values from -0.4375 to 0.4375
- w_value: bfloat16 [512, 512], replicated, may hold values from -0.25 to 0.25
- w_out: bfloat16 [512, 512], replicated, may hold values from -0.5 to 0.5
- ln1_gain: float32 [512], replicated, may hold values from 0.1 to 1.9
- ln1_bias: float32 [512], replicated, may hold values from -2.4 to 2.4
- w_up: bfloat16 [512, 1024], replicated, may hold values from -0.25 to 0.25
- b_up: float32 [1024], replicated, may hold values from -3 to 3
- w_down: bfloat16 [1024, 512], replicated, may hold values from -0.25 to 0.25
- ln2_gain: float32 [512], replicated, may hold values from 0.1 to 1.9
- ln2_bias: float32 [512], replicated, may hold values from -2.4 to 2.4
Outputs:
- layer_out: float32 [65536, 512], P(('blk', 'head'))
Inputs may be any that keep to these rules, and one draw needn't show every extreme that they name: `pair_tiles`: each entry is q * 16 + k for a query block q and key block k of the two groups; the entries of one list are distinct. `pair_count`: every query group has some key group with 8 pairs used. `graph_ids`: values never fall along the nodes.
All inputs are finite; a program needn't handle non-finite values.
Results may differ from a plain program's by a relative error of at most 0.0085.
The roundings to bfloat16 on the way count: a program that leaves them out, or rounds other values in their place, can miss the bound.
Values may be sent and summed in bfloat16 or wider, within the bound.
No kernel may reach another device: no remote copies, remote signals or barrier semaphores. Data moves between devices by JAX's collectives and lax.ppermute only.
A program may use at most 192 MiB of HBM per device.

v0:
```python
import jax
import jax.numpy as jnp
from jax import lax
from jax.experimental import pallas as pl
from jax.experimental.pallas import tpu as pltpu
from jax.sharding import Mesh
from jax.sharding import PartitionSpec as P

F32 = jnp.float32
BF16 = jnp.bfloat16

AXES = ("zhi", "zlo", "ylo", "yhi", "x", "core")
SLAB = ("zlo", "ylo", "yhi", "x", "core")
D = 512
FF = 1024
HEADS = 8
HEAD_DIM = 64
COUPLES = HEADS // 2
ROWS = 128
MEMBERS = 16
SLAB_GROUPS = 4
SLAB_BLOCKS = 64
CAP = 8
TILE_ROWS = 8
TILE_COLS = 128
COL_TILES = D // TILE_COLS
SLOTS = 15
GULP = 5
MIB = 1024 * 1024
FLOOR = -1e30

SMEM = pl.BlockSpec(memory_space=pltpu.SMEM)
VMEM = pl.BlockSpec(memory_space=pltpu.VMEM)


def absorb(state, keys, values, query_ref, mask=None, bias=()):
    bias = bias or (None,)
    size = keys.shape[0] // len(bias)
    new = []
    for couple in range(COUPLES):
        top, total, accum = state[couple]
        cols = slice(couple * 2 * HEAD_DIM, (couple + 1) * 2 * HEAD_DIM)
        scores = [
            jnp.dot(keys[n * size : (n + 1) * size, cols], query_ref[couple], preferred_element_type=F32)
            for n in range(len(bias))
        ]
        if mask is not None:
            scores = [jnp.where(mask, scores[0], FLOOR)]
        new_top = top
        for part, shift in zip(scores, bias):
            best = jnp.max(part, axis=0, keepdims=True)
            new_top = jnp.maximum(new_top, best if shift is None else best + shift)
        decay = jnp.exp(top - new_top)
        total = total * decay
        probs = []
        for part, shift in zip(scores, bias):
            prob = jnp.exp(part - (new_top if shift is None else new_top - shift))
            total = total + jnp.sum(prob, axis=0, keepdims=True)
            probs.append(prob.astype(BF16))
        part = lax.dot_general(
            values[:, cols],
            jnp.concatenate(probs, axis=0),
            (((0,), (0,)), ((), ())),
            preferred_element_type=F32,
        )
        accum = jnp.concatenate(
            [
                accum[:HEAD_DIM] * decay[:, :ROWS] + part[:HEAD_DIM, :ROWS],
                accum[HEAD_DIM:] * decay[:, ROWS:] + part[HEAD_DIM:, ROWS:],
            ],
            axis=0,
        )
        new.append((new_top, total, accum))
    return new


def read_state(top_ref, total_ref, accum_ref):
    return [
        (
            top_ref[c : c + 1, :],
            total_ref[c : c + 1, :],
            accum_ref[c * 2 * HEAD_DIM : (c + 1) * 2 * HEAD_DIM, :],
        )
        for c in range(COUPLES)
    ]


def write_state(state, top_ref, total_ref, accum_ref):
    for c, (top, total, accum) in enumerate(state):
        top_ref[c : c + 1, :] = top
        total_ref[c : c + 1, :] = total
        accum_ref[c * 2 * HEAD_DIM : (c + 1) * 2 * HEAD_DIM, :] = accum


def project(x, weight_ref):
    return jnp.dot(x, weight_ref[...], preferred_element_type=F32).astype(BF16)


STATE_SHAPES = (
    jax.ShapeDtypeStruct((COUPLES, 2 * ROWS), F32),
    jax.ShapeDtypeStruct((COUPLES, 2 * ROWS), F32),
    jax.ShapeDtypeStruct((D, ROWS), F32),
)


def near_kernel(
    beside_ref, x_ref, across_ref, wq_ref, wk_ref, wv_ref, kid_ref, qid_ref, query_ref, top_ref, total_ref, accum_ref
):
    x = x_ref[...]
    query = jnp.dot(x, wq_ref[...], preferred_element_type=F32).astype(BF16).astype(F32)
    query_t = (query.T * (1.0 / 8.0)).astype(BF16)
    zero = jnp.zeros((HEAD_DIM, ROWS), BF16)
    for couple in range(COUPLES):
        at = couple * 2 * HEAD_DIM
        first = query_t[at : at + HEAD_DIM]
        second = query_t[at + HEAD_DIM : at + 2 * HEAD_DIM]
        query_ref[couple] = jnp.concatenate(
            [jnp.concatenate([first, zero], axis=1), jnp.concatenate([zero, second], axis=1)], axis=0
        )
    state = [
        (
            jnp.full((1, 2 * ROWS), FLOOR, F32),
            jnp.zeros((1, 2 * ROWS), F32),
            jnp.zeros((2 * HEAD_DIM, ROWS), F32),
        )
    ] * COUPLES
    sources = jnp.concatenate([beside_ref[...], x, across_ref[...]], axis=0)
    mask = kid_ref[...] == qid_ref[...]
    state = absorb(state, project(sources, wk_ref), project(sources, wv_ref), query_ref, mask)
    write_state(state, top_ref, total_ref, accum_ref)


def near(beside, x, across, wq, wk, wv, key_ids, query_ids):
    return pl.pallas_call(
        near_kernel,
        out_shape=(jax.ShapeDtypeStruct((COUPLES, 2 * HEAD_DIM, 2 * ROWS), BF16),) + STATE_SHAPES,
        compiler_params=pltpu.CompilerParams(vmem_limit_bytes=32 * MIB),
        cost_estimate=pl.CostEstimate(flops=10**9, bytes_accessed=3 * MIB, transcendentals=400000),
        name="near",
    )(beside, x, across, wq, wk, wv, key_ids, query_ids)


def pack_kernel(x_ref, tiles_ref, counts_ref, out_ref):
    x = x_ref[...].astype(F32)
    used = lax.broadcasted_iota(jnp.int32, tiles_ref.shape, 0) < counts_ref[...]
    codes = jnp.where(used, tiles_ref[...], MEMBERS * MEMBERS).astype(F32)
    codes = jnp.concatenate([codes, jnp.zeros((CAP, TILE_COLS - codes.shape[1]), F32)], axis=1)
    for n in range(SLAB_BLOCKS):
        row, col = n // COL_TILES * TILE_ROWS, n % COL_TILES * TILE_COLS
        tile = x[row : row + TILE_ROWS, col : col + TILE_COLS]
        out_ref[n] = jnp.concatenate([tile, codes], axis=0).astype(BF16)


def pack(x, pair_tiles, pair_count):
    return pl.pallas_call(
        pack_kernel,
        out_shape=jax.ShapeDtypeStruct((SLAB_BLOCKS, TILE_ROWS + CAP, TILE_COLS), BF16),
        compiler_params=pltpu.CompilerParams(vmem_limit_bytes=60 * MIB),
        name="pack",
    )(x, pair_tiles[0].T, pair_count)


def select_kernel(at_ref, list_ref, *refs):
    sources, out_ref, all_ref = refs[:-2], refs[-2], refs[-1]
    at = 0
    for source in sources:
        all_ref[at : at + source.shape[0]] = source[...]
        at += source.shape[0]

    def one(dest, carry):
        at = at_ref[dest]
        for slot in range(SLOTS):
            out_ref[dest, slot] = all_ref[list_ref[at + slot]]
        return carry

    lax.fori_loop(0, SLAB_BLOCKS, one, 0, unroll=4)


def select(at, pairs, gathered):
    return pl.pallas_call(
        select_kernel,
        in_specs=[SMEM] * 2 + [VMEM] * len(gathered),
        out_specs=VMEM,
        out_shape=jax.ShapeDtypeStruct((SLAB_BLOCKS, SLOTS, TILE_ROWS, TILE_COLS), BF16),
        scratch_shapes=[pltpu.VMEM((sum(g.shape[0] for g in gathered), TILE_ROWS, TILE_COLS), BF16)],
        compiler_params=pltpu.CompilerParams(vmem_limit_bytes=32 * MIB),
        cost_estimate=pl.CostEstimate(flops=0, bytes_accessed=8 * MIB, transcendentals=0),
        name="select",
    )(at, pairs, *gathered)


def gather_block(held_ref, slot):
    rows = []
    for r in range(ROWS // TILE_ROWS):
        tiles = [held_ref[r * COL_TILES + c, slot].astype(F32) for c in range(COL_TILES)]
        rows.append(jnp.concatenate(tiles, axis=1))
    return jnp.concatenate(rows, axis=0).astype(BF16)


def far_steps(count, held_ref, query_ref, wk_ref, wv_ref, state_refs):
    def step(i, carry):
        slots = [GULP * i + u for u in range(GULP)]
        x = jnp.concatenate([gather_block(held_ref, slot) for slot in slots], axis=0)
        bias = [jnp.where(slot < count, 0.0, FLOOR).astype(F32) for slot in slots]
        state = read_state(*state_refs)
        state = absorb(state, project(x, wk_ref), project(x, wv_ref), query_ref, bias=bias)
        write_state(state, *state_refs)
        return carry

    lax.fori_loop(0, (count + GULP - 1) // GULP, step, 0)


def far_kernel(
    count_ref, held_ref, query_ref, wk_ref, wv_ref, top_in, total_in, accum_in, top_ref, total_ref, accum_ref
):
    top_ref[...] = top_in[...]
    total_ref[...] = total_in[...]
    accum_ref[...] = accum_in[...]
    far_steps(count_ref[0], held_ref, query_ref, wk_ref, wv_ref, (top_ref, total_ref, accum_ref))


def far(count, held, query, wk, wv, state):
    return pl.pallas_call(
        far_kernel,
        in_specs=[SMEM] + [VMEM] * 7,
        out_specs=(VMEM,) * 3,
        out_shape=STATE_SHAPES,
        compiler_params=pltpu.CompilerParams(vmem_limit_bytes=32 * MIB),
        name="far",
    )(count, held, query, wk, wv, *state)


def layer_norm(value, gain, bias):
    mean = jnp.mean(value, -1, keepdims=True)
    centred = value - mean
    spread = jnp.mean(centred * centred, -1, keepdims=True)
    return centred * lax.rsqrt(spread + 1e-05) * gain + bias


def finish_kernel(
    count_ref,
    held_ref,
    query_ref,
    wk_ref,
    wv_ref,
    top_in,
    total_in,
    accum_in,
    x_ref,
    g1_ref,
    b1_ref,
    b_up_ref,
    g2_ref,
    b2_ref,
    w_out_hbm,
    w_up_hbm,
    w_down_hbm,
    out_ref,
    top_ref,
    total_ref,
    accum_ref,
    w_out_ref,
    w_up_ref,
    w_down_ref,
    sems,
):
    weights = ((w_out_hbm, w_out_ref), (w_up_hbm, w_up_ref), (w_down_hbm, w_down_ref))
    copies = [pltpu.make_async_copy(a, b, sems.at[n]) for n, (a, b) in enumerate(weights)]
    for copy in copies:
        copy.start()
    far_kernel(
        count_ref,
        held_ref,
        query_ref,
        wk_ref,
        wv_ref,
        top_in,
        total_in,
        accum_in,
        top_ref,
        total_ref,
        accum_ref,
    )
    columns = []
    for head in range(HEADS):
        lanes = slice(head % 2 * ROWS, (head % 2 + 1) * ROWS)
        total = total_ref[head // 2 : head // 2 + 1, lanes]
        accum = accum_ref[head * HEAD_DIM : (head + 1) * HEAD_DIM, :]
        columns.append((accum / total).astype(BF16))
    attended_t = jnp.concatenate(columns, axis=0)
    copies[0].wait()
    mixed = x_ref[...].astype(F32) + lax.dot_general(
        attended_t, w_out_ref[...], (((0,), (0,)), ((), ())), preferred_element_type=F32
    )
    normed = layer_norm(mixed, g1_ref[...], b1_ref[...]).astype(BF16)
    copies[1].wait()
    hidden = jnp.maximum(
        jnp.dot(normed, w_up_ref[...], preferred_element_type=F32) + b_up_ref[...], 0.0
    ).astype(BF16)
    copies[2].wait()
    second = normed.astype(F32) + jnp.dot(hidden, w_down_ref[...], preferred_element_type=F32)
    out_ref[...] = layer_norm(second, g2_ref[...], b2_ref[...])


def finish(count, held, query, wk, wv, state, x, g1, b1, b_up, g2, b2, w_out, w_up, w_down):
    hbm = pl.BlockSpec(memory_space=pltpu.HBM)
    return pl.pallas_call(
        finish_kernel,
        in_specs=[SMEM] + [VMEM] * 13 + [hbm] * 3,
        out_specs=(VMEM,) * 4,
        out_shape=(jax.ShapeDtypeStruct((ROWS, D), F32),) + STATE_SHAPES,
        scratch_shapes=[
            pltpu.VMEM((D, D), BF16),
            pltpu.VMEM((D, FF), BF16),
            pltpu.VMEM((FF, D), BF16),
            pltpu.SemaphoreType.DMA((3,)),
        ],
        compiler_params=pltpu.CompilerParams(vmem_limit_bytes=44 * MIB),
        cost_estimate=pl.CostEstimate(flops=4 * 10**9, bytes_accessed=8 * MIB, transcendentals=10**6),
        name="finish",
    )(
        count,
        held,
        query,
        wk,
        wv,
        *state,
        x,
        g1[None],
        b1[None],
        b_up[None],
        g2[None],
        b2[None],
        w_out,
        w_up,
        w_down,
    )


def pair_lists(held, z_high, core):
    size = held.shape[1]
    planes = lax.axis_size("zhi")
    slot = jnp.arange(size, dtype=jnp.int32)
    key_group = slot % (size // CAP)
    distance = z_high - key_group // SLAB_GROUPS
    distance = jnp.where(core == 0, distance, -distance) % planes
    query_index = held // MEMBERS
    key_slot = (distance * SLAB_BLOCKS + key_group % SLAB_GROUPS * MEMBERS)[None, :] + held % MEMBERS
    ahead = (query_index[:, None, :] < query_index[:, :, None]) | (
        (query_index[:, None, :] == query_index[:, :, None]) & (slot[None, None, :] < slot[None, :, None])
    )
    place = jnp.sum(ahead.astype(jnp.int32), axis=-1)
    pairs = jnp.sum(jnp.where(place[:, None, :] == slot[None, :, None], key_slot[:, None, :], 0), axis=-1)
    pairs = jnp.concatenate([pairs.reshape(-1), jnp.zeros((SLOTS,), jnp.int32)])
    member = jnp.arange(MEMBERS, dtype=jnp.int32)[None, :, None]
    start = jnp.sum((query_index[:, None, :] < member).astype(jnp.int32), axis=-1)
    count = jnp.sum((query_index[:, None, :] == member).astype(jnp.int32), axis=-1)
    start = start + size * jnp.arange(SLAB_GROUPS, dtype=jnp.int32)[:, None]
    return start.reshape(-1), count.reshape(-1), pairs


def gather_rings(tiles):
    size = lax.axis_size("zhi")

    def move(value, step):
        pairs = [
            (2 * z + core, 2 * ((z + (step if core == 0 else -step)) % size) + core)
            for z in range(size)
            for core in range(2)
        ]
        return lax.ppermute(value, ("zhi", "core"), pairs)

    ahead, behind = [tiles], [tiles]
    for step in range(size // 2):
        ahead.append(move(ahead[-1], 1))
        if step < (size - 1) // 2:
            behind.append(move(behind[-1], -1))
    return ahead + behind[:0:-1]


def swap(x, pairs):
    return lax.ppermute(x, AXES, [p for a, b in pairs for p in ((a, b), (b, a))])


def on_device(
    node_feats,
    graph_ids,
    pair_tiles,
    pair_count,
    w_query,
    w_key,
    w_value,
    w_out,
    ln1_gain,
    ln1_bias,
    w_up,
    b_up,
    w_down,
    ln2_gain,
    ln2_bias,
):
    z_high, own = lax.axis_index("zhi"), lax.axis_index(SLAB)
    devices = lax.axis_size(AXES)

    def exchange(value):
        return lax.all_to_all(value, SLAB, split_axis=0, concat_axis=0, tiled=True)

    got = exchange(pack(node_feats, pair_tiles, pair_count))
    beside = swap(node_feats, [(i, i + 1) for i in range(0, devices, 2)])
    across = swap(node_feats, [(i, i + 1) for i in range(1, devices - 1, 2)])
    tiles, beside, across = lax.optimization_barrier((got[:, :TILE_ROWS], beside, across))
    core = lax.axis_index("core")
    gathered = gather_rings(tiles)
    codes = got[::MEMBERS, TILE_ROWS:, : pair_tiles.shape[1]].astype(jnp.int32)
    start, count, pairs = pair_lists(codes.reshape(SLAB_GROUPS, -1), z_high, core)

    def mine(value):
        return lax.dynamic_slice_in_dim(value, own, 1, 0)

    fill = jnp.full((ROWS,), -1, jnp.int32)
    ids = jnp.concatenate([fill, graph_ids, fill])
    key_ids = lax.dynamic_slice_in_dim(ids, (z_high * SLAB_BLOCKS + own) * ROWS, 3 * ROWS, 0)
    query_ids = jnp.tile(key_ids[ROWS : 2 * ROWS], 2)[None, :]
    turned = key_ids.reshape(3, ROWS)[::-1].reshape(-1)
    key_ids = jnp.where(core == 0, turned, key_ids)
    query, *state = near(
        beside, node_feats, across, w_query, w_key, w_value, key_ids[:, None], query_ids
    )

    def fetch(at):
        held = exchange(select(start + jnp.minimum(at, count), pairs, gathered))
        return jnp.clip(mine(count) - at, 0, SLOTS), held

    def close(part, held, state):
        return finish(
            part,
            held,
            query,
            w_key,
            w_value,
            state,
            node_feats,
            ln1_gain,
            ln1_bias,
            b_up,
            ln2_gain,
            ln2_bias,
            w_out,
            w_up,
            w_down,
        )

    part, held = fetch(jnp.int32(0))
    out, *state = close(part, held, state)
    most = jnp.max(count)

    def go_on(state):
        def more(carry):
            at, state = carry
            part, held = fetch(at)
            return at + SLOTS, tuple(far(part, held, query, w_key, w_value, state))

        _, state = lax.while_loop(lambda carry: carry[0] < most, more, (jnp.int32(SLOTS), state))
        return close(jnp.zeros_like(part), held, state)[0]

    return lax.cond(most > SLOTS, go_on, lambda state: out, tuple(state))


def solution(mesh):
    inner = Mesh(mesh.devices.reshape(-1, 2, 2, 2, 4, 2), AXES)
    blk = ("zhi", "zlo", "ylo")
    in_specs = (P(AXES, None), P(), P(blk, None, None), P(blk, None)) + (P(),) * 11
    return jax.shard_map(
        on_device, mesh=inner, in_specs=in_specs, out_specs=P(AXES, None), check_vma=False
    )
```

profile of v0, /device:TPU:1, one launch (start us, length us, event | category | flops | bytes accessed | tf_op | source)
XLA Modules:
  0.0 119.1 jit_solution(5063540177322124106)
XLA Ops:
  0.0 1.6 %pack.1 = bf16[64,16,128]{2,1,0:T(8,128)(2,1)} custom-call(bf16[128,512]{1,0:T(8,128)(2,1)} %x_ref.5, s32[8,32]{1,0:T(8,128)} %bitcast.26, s32[1,32]{1,0:T(1,128)} %counts_ref.1), custom_call_target="tpu_custom_call" | custom-call | tf_op jit(solution)/shard_map/pack/pallas_call | solution.py:155
  1.6 10.9 %all-to-all-start.1 = ((bf16[64,16,128]{2,1,0:T(8,128)(2,1)}), bf16[64,16,128]{2,1,0:T(8,128)(2,1)S(1)}, u32[]{:S(2)}, u32[]{:S(2)}) async-start(bf16[64,16,128]{2,1,0:T(8,128)(2,1)} %pack.1), calls=%async_computation.1 | async-start | bytes 524288 | tf_op jit(solution)/shard_map/all_to_all | solution.py:406
  12.6 2.5 %collective-permute-start = (bf16[128,512]{1,0:T(8,128)(2,1)}, bf16[128,512]{1,0:T(8,128)(2,1)S(1)}, u32[]{:S(2)}, u32[]{:S(2)}) collective-permute-start(bf16[128,512]{1,0:T(8,128)(2,1)} %x_ref.5), channel_id=1, source_target_pairs={{0,1},{1,0},{2,3},{3,2},{4,5},{5,4},{6,7},{7,6},{8,9},{9,8},{10,11... | collective-permute-start | bytes 393224 | tf_op jit(solution)/shard_map/ppermute | solution.py:382
  15.1 3.1 %collective-permute-start.1 = (bf16[128,512]{1,0:T(8,128)(2,1)}, bf16[128,512]{1,0:T(8,128)(2,1)S(1)}, u32[]{:S(2)}, u32[]{:S(2)}) collective-permute-start(bf16[128,512]{1,0:T(8,128)(2,1)} %x_ref.5), channel_id=1, source_target_pairs={{1,2},{2,1},{3,4},{4,3},{5,6},{6,5},{7,8},{8,7},{9,10},{10,9},{11,... | collective-permute-start | bytes 393224 | tf_op jit(solution)/shard_map/ppermute | solution.py:382
  18.3 4.2 %all-to-all-done.1 = bf16[64,16,128]{2,1,0:T(8,128)(2,1)S(1)} async-done(((bf16[64,16,128]{2,1,0:T(8,128)(2,1)}), bf16[64,16,128]{2,1,0:T(8,128)(2,1)S(1)}, u32[]{:S(2)}, u32[]{:S(2)}) %all-to-all-start.1) | async-done | bytes 262176 | tf_op jit(solution)/shard_map/all_to_all | solution.py:406
  22.5 0.7 slice.12.refs_0_
  23.2 0.0 collective-permute-done.beside_ref
  23.2 0.0 collective-permute-done.1.across_ref
  23.2 10.0 %collective-permute-start.2 = (bf16[64,8,128]{2,1,0:T(8,128)(2,1)}, bf16[64,8,128]{2,1,0:T(8,128)(2,1)}, u32[]{:S(2)}, u32[]{:S(2)}) collective-permute-start(bf16[64,8,128]{2,1,0:T(8,128)(2,1)} %slice.12.refs_0_), channel_id=1, source_target_pairs={{0,64},{1,449},{64,128},{65,1},{128,192},{129,65},{192,256},{193,1... | collective-permute-start | bytes 393224 | tf_op jit(solution)/shard_map/ppermute | solution.py:371
  33.1 1.9 %collective-permute-start.6 = (bf16[64,8,128]{2,1,0:T(8,128)(2,1)}, bf16[64,8,128]{2,1,0:T(8,128)(2,1)}, u32[]{:S(2)}, u32[]{:S(2)}) collective-permute-start(bf16[64,8,128]{2,1,0:T(8,128)(2,1)} %slice.12.refs_0_), channel_id=1, source_target_pairs={{0,448},{1,65},{64,0},{65,129},{128,64},{129,193},{192,128},{193,2... | collective-permute-start | bytes 393224 | tf_op jit(solution)/shard_map/ppermute | solution.py:371
  35.1 0.1 reshape.192
  35.2 0.2 convert_reduce_fusion.1
  35.4 0.6 reshape.187
  36.0 0.1 broadcast_add_fusion
  36.1 0.6 add.129
  36.7 0.0 collective-permute-done.2.refs_1_
  36.7 5.8 %collective-permute-start.3 = (bf16[64,8,128]{2,1,0:T(8,128)(2,1)}, bf16[64,8,128]{2,1,0:T(8,128)(2,1)}, u32[]{:S(2)}, u32[]{:S(2)}) collective-permute-start(bf16[64,8,128]{2,1,0:T(8,128)(2,1)} %collective-permute-done.2.refs_1_), channel_id=1, source_target_pairs={{0,64},{1,449},{64,128},{65,1},{128,192},{129,65},{192,256},{193,1... | collective-permute-start | bytes 393224 | tf_op jit(solution)/shard_map/ppermute | solution.py:371
  42.5 0.5 convert_reduce_fusion
  43.0 0.0 collective-permute-done.6.refs_7_
  43.0 1.9 %collective-permute-start.7 = (bf16[64,8,128]{2,1,0:T(8,128)(2,1)}, bf16[64,8,128]{2,1,0:T(8,128)(2,1)}, u32[]{:S(2)}, u32[]{:S(2)}) collective-permute-start(bf16[64,8,128]{2,1,0:T(8,128)(2,1)} %collective-permute-done.6.refs_7_), channel_id=1, source_target_pairs={{0,448},{1,65},{64,0},{65,129},{128,64},{129,193},{192,128},{193,2... | collective-permute-start | bytes 393224 | tf_op jit(solution)/shard_map/ppermute | solution.py:371
  44.9 1.0 collective-permute-done.3.refs_2_
  46.0 5.9 %collective-permute-start.4 = (bf16[64,8,128]{2,1,0:T(8,128)(2,1)}, bf16[64,8,128]{2,1,0:T(8,128)(2,1)}, u32[]{:S(2)}, u32[]{:S(2)}) collective-permute-start(bf16[64,8,128]{2,1,0:T(8,128)(2,1)} %collective-permute-done.3.refs_2_), channel_id=1, source_target_pairs={{0,64},{1,449},{64,128},{65,1},{128,192},{129,65},{192,256},{193,1... | collective-permute-start | bytes 393224 | tf_op jit(solution)/shard_map/ppermute | solution.py:371
  51.9 0.2 select_reduce_fusion
  52.1 2.8 %collective-permute-done.7.refs_6_ = bf16[64,8,128]{2,1,0:T(8,128)(2,1)} collective-permute-done((bf16[64,8,128]{2,1,0:T(8,128)(2,1)}, bf16[64,8,128]{2,1,0:T(8,128)(2,1)}, u32[]{:S(2)}, u32[]{:S(2)}) %collective-permute-start.7) | collective-permute-done | bytes 131104 | tf_op jit(solution)/shard_map/ppermute | solution.py:371
  54.9 1.9 %collective-permute-start.8 = (bf16[64,8,128]{2,1,0:T(8,128)(2,1)}, bf16[64,8,128]{2,1,0:T(8,128)(2,1)}, u32[]{:S(2)}, u32[]{:S(2)}) collective-permute-start(bf16[64,8,128]{2,1,0:T(8,128)(2,1)} %collective-permute-done.7.refs_6_), channel_id=1, source_target_pairs={{0,448},{1,65},{64,0},{65,129},{128,64},{129,193},{192,128},{193,2... | collective-permute-start | bytes 393224 | tf_op jit(solution)/shard_map/ppermute | solution.py:371
  56.8 0.2 collective-permute-done.4.refs_3_
  57.0 5.3 %collective-permute-start.5 = (bf16[64,8,128]{2,1,0:T(8,128)(2,1)}, bf16[64,8,128]{2,1,0:T(8,128)(2,1)}, u32[]{:S(2)}, u32[]{:S(2)}) collective-permute-start(bf16[64,8,128]{2,1,0:T(8,128)(2,1)} %collective-permute-done.4.refs_3_), channel_id=1, source_target_pairs={{0,64},{1,449},{64,128},{65,1},{128,192},{129,65},{192,256},{193,1... | collective-permute-start | bytes 393224 | tf_op jit(solution)/shard_map/ppermute | solution.py:371
  62.3 0.6 minimum_add_fusion.1.at_ref
  62.9 1.1 collective-permute-done.8.refs_5_
  64.1 4.1 %collective-permute-done.5.refs_4_ = bf16[64,8,128]{2,1,0:T(8,128)(2,1)} collective-permute-done((bf16[64,8,128]{2,1,0:T(8,128)(2,1)}, bf16[64,8,128]{2,1,0:T(8,128)(2,1)}, u32[]{:S(2)}, u32[]{:S(2)}) %collective-permute-start.5) | collective-permute-done | bytes 131104 | tf_op jit(solution)/shard_map/ppermute | solution.py:371
  68.2 3.7 %select.78 = bf16[64,15,8,128]{3,2,1,0:T(8,128)(2,1)} custom-call(s32[64]{0:T(128)S(1)} %minimum_add_fusion.1.at_ref, s32[1039]{0:T(1024)S(1)} %concatenate.6.list_ref, bf16[64,8,128]{2,1,0:T(8,128)(2,1)} %slice.12.refs_0_, bf16[64,8,128]{2,1,0:T(8,128)(2,1)} %collective-permute-done.2.refs_1_, bf16[64,8,128]{2,1,0:T(8,128)(2,1)} %collective-permute-done.3.refs_2_, ...), custom_call_target="tpu_custom_call" | custom-call | bytes 8388608 | tf_op jit(solution)/shard_map/select/pallas_call | solution.py:180
  71.9 0.0 copy-start.3
  71.9 0.0 copy-start
  71.9 0.0 copy-start.1
  71.9 0.0 copy-start.2
  71.9 0.0 copy-start.4
  71.9 12.9 %all-to-all-start.2 = ((bf16[64,15,8,128]{3,2,1,0:T(8,128)(2,1)}), bf16[64,15,8,128]{3,2,1,0:T(8,128)(2,1)}, u32[]{:S(2)}, u32[]{:S(2)}) async-start(bf16[64,15,8,128]{3,2,1,0:T(8,128)(2,1)} %select.78), calls=%async_computation.2 | async-start | bytes 3932160 | tf_op jit(solution)/shard_map/all_to_all | solution.py:406
  84.9 0.0 copy-done.3
  84.9 0.1 fusion.8
  85.0 0.1 bitcast_select_fusion
  85.1 0.1 broadcast_in_dim.71.kid_ref
  85.2 0.0 copy-start.6
  85.2 0.0 copy-start.8
  85.3 0.0 copy-start.10
  85.3 0.0 copy-start.12
  85.3 0.0 copy-start.14
  85.3 0.0 copy-start.16
  85.3 0.1 fusion.3
  85.4 1.3 %dynamic_slice.11 = s32[1]{0:T(128)} dynamic-slice(s32[64]{0:T(128)} %reshape.187, s32[]{:T(128)S(6)} %select_n.97), dynamic_slice_sizes={1} | dynamic-slice | bytes 12 | tf_op jit(solution)/shard_map/dynamic_slice | solution.py:418
  86.7 0.7 reduce_max.9
  88.7 0.0 copy-done
  88.7 0.0 copy-done.1
  88.7 0.0 copy-done.2
  88.7 0.0 copy-done.4
  88.8 2.1 %near.1 = (bf16[4,128,256]{2,1,0:T(8,128)(2,1)S(1)}, f32[4,256]{1,0:T(4,128)S(1)}, f32[4,256]{1,0:T(4,128)S(1)}, f32[512,128]{1,0:T(8,128)S(1)}) custom-call(bf16[128,512]{1,0:T(8,128)(2,1)S(1)} %collective-permute-done.beside_ref, bf16[128,512]{1,0:T(8,128)(2,1)S(1)} %copy-done.4, bf16[128,512]{1,0:T(8,128)(2,1)S(1)} %collective-permute-done.1.across_ref, ...), custom_call_target="tpu_custom_call" | custom-call | flops 1000000000 | bytes 3145728 | tf_op jit(solution)/shard_map/near/pallas_call | solution.py:134
  90.9 21.8 %all-to-all-done.2.held_ref = bf16[64,15,8,128]{3,2,1,0:T(8,128)(2,1)} async-done(((bf16[64,15,8,128]{3,2,1,0:T(8,128)(2,1)}), bf16[64,15,8,128]{3,2,1,0:T(8,128)(2,1)}, u32[]{:S(2)}, u32[]{:S(2)}) %all-to-all-start.2) | async-done | bytes 1966112 | tf_op jit(solution)/shard_map/all_to_all | solution.py:406
  112.6 0.0 copy-done.6
  112.6 0.0 copy-done.8
  112.6 0.0 copy-done.10
  112.6 0.0 copy-done.12
  112.6 0.0 copy-done.14
  112.6 0.0 copy-done.16
  112.7 6.0 %finish.3 = (f32[128,512]{1,0:T(8,128)}, f32[4,256]{1,0:T(4,128)S(1)}, f32[4,256]{1,0:T(4,128)S(1)}, f32[512,128]{1,0:T(8,128)S(1)}) custom-call(s32[1]{0:T(128)S(6)} %min.29.count_ref, bf16[64,15,8,128]{3,2,1,0:T(8,128)(2,1)} %all-to-all-done.2.held_ref, bf16[4,128,256]{2,1,0:T(8,128)(2,1)S(1)} %get-tuple-element.337.query_ref, ...), custom_call_target="tpu_custom_call" | custom-call | flops 4000000000 | bytes 8388608 | tf_op jit(solution)/shard_map/finish/pallas_call | solution.py:307
  118.7 0.2 conditional.1
  (11 shorter events, 0.1 us)
Async XLA Ops:
  1.6 20.9 %all-to-all-start.1 = ((bf16[64,16,128]{2,1,0:T(8,128)(2,1)}), bf16[64,16,128]{2,1,0:T(8,128)(2,1)S(1)}, u32[]{:S(2)}, u32[]{:S(2)}) async-start(bf16[64,16,128]{2,1,0:T(8,128)(2,1)} %pack.1), calls=%async_computation.1 | async-start | bytes 524288 | tf_op jit(solution)/shard_map/all_to_all | solution.py:406
  12.6 10.6 %collective-permute-start = (bf16[128,512]{1,0:T(8,128)(2,1)}, bf16[128,512]{1,0:T(8,128)(2,1)S(1)}, u32[]{:S(2)}, u32[]{:S(2)}) collective-permute-start(bf16[128,512]{1,0:T(8,128)(2,1)} %x_ref.5), channel_id=1, source_target_pairs={{0,1},{1,0},{2,3},{3,2},{4,5},{5,4},{6,7},{7,6},{8,9},{9,8},{10,11... | collective-permute-start | bytes 393224 | tf_op jit(solution)/shard_map/ppermute | solution.py:382
  15.1 8.1 %collective-permute-start.1 = (bf16[128,512]{1,0:T(8,128)(2,1)}, bf16[128,512]{1,0:T(8,128)(2,1)S(1)}, u32[]{:S(2)}, u32[]{:S(2)}) collective-permute-start(bf16[128,512]{1,0:T(8,128)(2,1)} %x_ref.5), channel_id=1, source_target_pairs={{1,2},{2,1},{3,4},{4,3},{5,6},{6,5},{7,8},{8,7},{9,10},{10,9},{11,... | collective-permute-start | bytes 393224 | tf_op jit(solution)/shard_map/ppermute | solution.py:382
  23.2 13.5 %collective-permute-start.2 = (bf16[64,8,128]{2,1,0:T(8,128)(2,1)}, bf16[64,8,128]{2,1,0:T(8,128)(2,1)}, u32[]{:S(2)}, u32[]{:S(2)}) collective-permute-start(bf16[64,8,128]{2,1,0:T(8,128)(2,1)} %slice.12.refs_0_), channel_id=1, source_target_pairs={{0,64},{1,449},{64,128},{65,1},{128,192},{129,65},{192,256},{193,1... | collective-permute-start | bytes 393224 | tf_op jit(solution)/shard_map/ppermute | solution.py:371
  33.1 9.9 %collective-permute-start.6 = (bf16[64,8,128]{2,1,0:T(8,128)(2,1)}, bf16[64,8,128]{2,1,0:T(8,128)(2,1)}, u32[]{:S(2)}, u32[]{:S(2)}) collective-permute-start(bf16[64,8,128]{2,1,0:T(8,128)(2,1)} %slice.12.refs_0_), channel_id=1, source_target_pairs={{0,448},{1,65},{64,0},{65,129},{128,64},{129,193},{192,128},{193,2... | collective-permute-start | bytes 393224 | tf_op jit(solution)/shard_map/ppermute | solution.py:371
  36.7 9.3 %collective-permute-start.3 = (bf16[64,8,128]{2,1,0:T(8,128)(2,1)}, bf16[64,8,128]{2,1,0:T(8,128)(2,1)}, u32[]{:S(2)}, u32[]{:S(2)}) collective-permute-start(bf16[64,8,128]{2,1,0:T(8,128)(2,1)} %collective-permute-done.2.refs_1_), channel_id=1, source_target_pairs={{0,64},{1,449},{64,128},{65,1},{128,192},{129,65},{192,256},{193,1... | collective-permute-start | bytes 393224 | tf_op jit(solution)/shard_map/ppermute | solution.py:371
  43.0 11.9 %collective-permute-start.7 = (bf16[64,8,128]{2,1,0:T(8,128)(2,1)}, bf16[64,8,128]{2,1,0:T(8,128)(2,1)}, u32[]{:S(2)}, u32[]{:S(2)}) collective-permute-start(bf16[64,8,128]{2,1,0:T(8,128)(2,1)} %collective-permute-done.6.refs_7_), channel_id=1, source_target_pairs={{0,448},{1,65},{64,0},{65,129},{128,64},{129,193},{192,128},{193,2... | collective-permute-start | bytes 393224 | tf_op jit(solution)/shard_map/ppermute | solution.py:371
  46.0 11.0 %collective-permute-start.4 = (bf16[64,8,128]{2,1,0:T(8,128)(2,1)}, bf16[64,8,128]{2,1,0:T(8,128)(2,1)}, u32[]{:S(2)}, u32[]{:S(2)}) collective-permute-start(bf16[64,8,128]{2,1,0:T(8,128)(2,1)} %collective-permute-done.3.refs_2_), channel_id=1, source_target_pairs={{0,64},{1,449},{64,128},{65,1},{128,192},{129,65},{192,256},{193,1... | collective-permute-start | bytes 393224 | tf_op jit(solution)/shard_map/ppermute | solution.py:371
  54.9 9.2 %collective-permute-start.8 = (bf16[64,8,128]{2,1,0:T(8,128)(2,1)}, bf16[64,8,128]{2,1,0:T(8,128)(2,1)}, u32[]{:S(2)}, u32[]{:S(2)}) collective-permute-start(bf16[64,8,128]{2,1,0:T(8,128)(2,1)} %collective-permute-done.7.refs_6_), channel_id=1, source_target_pairs={{0,448},{1,65},{64,0},{65,129},{128,64},{129,193},{192,128},{193,2... | collective-permute-start | bytes 393224 | tf_op jit(solution)/shard_map/ppermute | solution.py:371
  57.0 11.2 %collective-permute-start.5 = (bf16[64,8,128]{2,1,0:T(8,128)(2,1)}, bf16[64,8,128]{2,1,0:T(8,128)(2,1)}, u32[]{:S(2)}, u32[]{:S(2)}) collective-permute-start(bf16[64,8,128]{2,1,0:T(8,128)(2,1)} %collective-permute-done.4.refs_3_), channel_id=1, source_target_pairs={{0,64},{1,449},{64,128},{65,1},{128,192},{129,65},{192,256},{193,1... | collective-permute-start | bytes 393224 | tf_op jit(solution)/shard_map/ppermute | solution.py:371
  71.9 13.0 %copy-start.3 = (s32[65536]{0:T(1024)S(1)}, s32[65536]{0:T(1024)}, u32[]{:S(2)}) copy-start(s32[65536]{0:T(1024)} %param.20) | copy-start | bytes 786436
  71.9 16.8 %copy-start = (bf16[512,512]{1,0:T(8,128)(2,1)S(1)}, bf16[512,512]{1,0:T(8,128)(2,1)}, u32[]{:S(2)}) copy-start(bf16[512,512]{1,0:T(8,128)(2,1)} %wq_ref.1) | copy-start | bytes 1572868
  71.9 16.8 %copy-start.1 = (bf16[512,512]{1,0:T(8,128)(2,1)S(1)}, bf16[512,512]{1,0:T(8,128)(2,1)}, u32[]{:S(2)}) copy-start(bf16[512,512]{1,0:T(8,128)(2,1)} %wk_ref.3) | copy-start | bytes 1572868
  71.9 16.8 %copy-start.2 = (bf16[512,512]{1,0:T(8,128)(2,1)S(1)}, bf16[512,512]{1,0:T(8,128)(2,1)}, u32[]{:S(2)}) copy-start(bf16[512,512]{1,0:T(8,128)(2,1)} %wv_ref.3) | copy-start | bytes 1572868
  71.9 16.8 %copy-start.4 = (bf16[128,512]{1,0:T(8,128)(2,1)S(1)}, bf16[128,512]{1,0:T(8,128)(2,1)}, u32[]{:S(2)}) copy-start(bf16[128,512]{1,0:T(8,128)(2,1)} %x_ref.5) | copy-start | bytes 393220
  71.9 40.7 %all-to-all-start.2 = ((bf16[64,15,8,128]{3,2,1,0:T(8,128)(2,1)}), bf16[64,15,8,128]{3,2,1,0:T(8,128)(2,1)}, u32[]{:S(2)}, u32[]{:S(2)}) async-start(bf16[64,15,8,128]{3,2,1,0:T(8,128)(2,1)} %select.78), calls=%async_computation.2 | async-start | bytes 3932160 | tf_op jit(solution)/shard_map/all_to_all | solution.py:406
  85.2 27.4 %copy-start.6 = (bf16[512,512]{1,0:T(8,128)(2,1)S(1)}, bf16[512,512]{1,0:T(8,128)(2,1)}, u32[]{:S(2)}) copy-start(bf16[512,512]{1,0:T(8,128)(2,1)} %w_out_hbm.1) | copy-start | bytes 1572868
  85.2 27.4 %copy-start.8 = (f32[1024]{0:T(1024)S(1)}, f32[1024]{0:T(1024)}, u32[]{:S(2)}) copy-start(f32[1024]{0:T(1024)} %param.30) | copy-start | bytes 12292
  85.3 27.4 %copy-start.10 = (f32[512]{0:T(512)S(1)}, f32[512]{0:T(512)}, u32[]{:S(2)}) copy-start(f32[512]{0:T(512)} %param.27) | copy-start | bytes 6148
  85.3 27.4 %copy-start.12 = (f32[512]{0:T(512)S(1)}, f32[512]{0:T(512)}, u32[]{:S(2)}) copy-start(f32[512]{0:T(512)} %param.28) | copy-start | bytes 6148
  85.3 27.3 %copy-start.14 = (f32[512]{0:T(512)S(1)}, f32[512]{0:T(512)}, u32[]{:S(2)}) copy-start(f32[512]{0:T(512)} %param.32) | copy-start | bytes 6148
  85.3 27.3 %copy-start.16 = (f32[512]{0:T(512)S(1)}, f32[512]{0:T(512)}, u32[]{:S(2)}) copy-start(f32[512]{0:T(512)} %param.33) | copy-start | bytes 6148
where the time goes:
time: 120 us; the launch traced here: 119 us
  starting transfers between devices  62.1 us (52%)
  waiting for transfers between devices  35.3 us (29%)
  Pallas kernels  13.5 us (11%)
  local copies, waits for them, and re-layouts  3.41 us (3%)
  other arithmetic  2.68 us (2%)
  between operations  1.86 us (2%)
    ppermute x7, starting transfers between devices, move(): return lax.ppermute(value, ('zhi', 'core'), pairs)  32.7 us
    all_to_all x2, waiting for transfers between devices, exchange(): return lax.all_to_all(value, SLAB, split_axis=0, concat_axis=0, tiled=True)  26 us
    all_to_all x2, starting transfers between devices, exchange(): return lax.all_to_all(value, SLAB, split_axis=0, concat_axis=0, tiled=True)  23.8 us
    ppermute x7, waiting for transfers between devices, move(): return lax.ppermute(value, ('zhi', 'core'), pairs)  9.27 us
    pallas_call x1, Pallas kernels, finish(): pl.pallas_call(finish_kernel, in_specs=[SMEM] + [VMEM] * 13 + [hbm] * 3,...  5.99 us
    ppermute x2, starting transfers between devices, swap(): lax.ppermute(x, AXES, [p for a, b in pairs for p in ((a, b), (b, a))])  5.61 us
    pallas_call x1, Pallas kernels, select(): pl.pallas_call(select_kernel, in_specs=[SMEM] * 2 + [VMEM] * len(gathered...  3.75 us
  transfers between devices with their start and end apart: 11, of which 7 were waited for; matrix products, arithmetic and copies ran while one was open for 5% of the time, Pallas kernels for 2%

commit v1 on v0

--- a/solution.py
+++ b/solution.py
@@ -359,7 +359,7 @@
     return start.reshape(-1), count.reshape(-1), pairs
 
 
-def gather_rings(tiles):
+def gather_rings(tiles, codes):
     size = lax.axis_size("zhi")
 
     def move(value, step):
@@ -372,10 +372,12 @@
 
     ahead, behind = [tiles], [tiles]
     for step in range(size // 2):
+        if step == size // 2 - 1:
+            ahead[-1], codes = lax.optimization_barrier((ahead[-1], codes))
         ahead.append(move(ahead[-1], 1))
         if step < (size - 1) // 2:
             behind.append(move(behind[-1], -1))
-    return ahead + behind[:0:-1]
+    return ahead + behind[:0:-1], codes
 
 
 def swap(x, pairs):
@@ -410,8 +412,8 @@
     across = swap(node_feats, [(i, i + 1) for i in range(1, devices - 1, 2)])
     tiles, beside, across = lax.optimization_barrier((got[:, :TILE_ROWS], beside, across))
     core = lax.axis_index("core")
-    gathered = gather_rings(tiles)
     codes = got[::MEMBERS, TILE_ROWS:, : pair_tiles.shape[1]].astype(jnp.int32)
+    gathered, codes = gather_rings(tiles, codes)
     start, count, pairs = pair_lists(codes.reshape(SLAB_GROUPS, -1), z_high, core)
 
     def mine(value):

time: 120 us -> 123 us (1.025)
  Pallas kernels: 13.5 us -> 15.9 us
    pallas_call x1, Pallas kernels: 5.99 us -> 8.4 us  [finish(): pl.pallas_call(finish_kernel, in_specs=[SMEM] + [VMEM] * 13 + [hbm] * 3,...]
  transfers between devices with their start and end apart: 11 -> 11, of which waited for: 7 -> 6; matrix products, arithmetic and copies ran while one was open for 5% -> 5% of each run, Pallas kernels for 2% -> 2%
where the time goes in v1:
time: 123 us
  starting transfers between devices  63.1 us (51%)
  waiting for transfers between devices  35.4 us (29%)
  Pallas kernels  15.9 us (13%)
  local copies, waits for them, and re-layouts  3.34 us (3%)
  other arithmetic  2.68 us (2%)
  between operations  1.86 us (2%)
    ppermute x7, starting transfers between devices, move(): return lax.ppermute(value, ('zhi', 'core'), pairs)  33 us
    all_to_all x2, waiting for transfers between devices, exchange(): return lax.all_to_all(value, SLAB, split_axis=0, concat_axis=0, tiled=True)  26 us
    all_to_all x2, starting transfers between devices, exchange(): return lax.all_to_all(value, SLAB, split_axis=0, concat_axis=0, tiled=True)  24.5 us
    ppermute x7, waiting for transfers between devices, move(): return lax.ppermute(value, ('zhi', 'core'), pairs)  9.38 us
    pallas_call x1, Pallas kernels, finish(): pl.pallas_call(finish_kernel, in_specs=[SMEM] + [VMEM] * 13 + [hbm] * 3,...  8.4 us
    ppermute x2, starting transfers between devices, swap(): lax.ppermute(x, AXES, [p for a, b in pairs for p in ((a, b), (b, a))])  5.61 us
    pallas_call x1, Pallas kernels, select(): pl.pallas_call(select_kernel, in_specs=[SMEM] * 2 + [VMEM] * len(gathered...  3.75 us
  transfers between devices with their start and end apart: 11, of which 6 were waited for; matrix products, arithmetic and copies ran while one was open for 5% of the time, Pallas kernels for 2%

profile of v1, /device:TPU:1, one launch (start us, length us, event | category | flops | bytes accessed | tf_op | source)
XLA Modules:
  0.0 122.5 jit_solution(4491048316125939945)
XLA Ops:
  0.0 1.6 %pack.1 = bf16[64,16,128]{2,1,0:T(8,128)(2,1)} custom-call(bf16[128,512]{1,0:T(8,128)(2,1)} %x_ref.5, s32[8,32]{1,0:T(8,128)} %bitcast.26, s32[1,32]{1,0:T(1,128)} %counts_ref.1), custom_call_target="tpu_custom_call" | custom-call | tf_op jit(solution)/shard_map/pack/pallas_call | solution.py:155
  1.6 10.9 %all-to-all-start.1 = ((bf16[64,16,128]{2,1,0:T(8,128)(2,1)}), bf16[64,16,128]{2,1,0:T(8,128)(2,1)S(1)}, u32[]{:S(2)}, u32[]{:S(2)}) async-start(bf16[64,16,128]{2,1,0:T(8,128)(2,1)} %pack.1), calls=%async_computation.1 | async-start | bytes 524288 | tf_op jit(solution)/shard_map/all_to_all | solution.py:408
  12.6 2.5 %collective-permute-start = (bf16[128,512]{1,0:T(8,128)(2,1)}, bf16[128,512]{1,0:T(8,128)(2,1)S(1)}, u32[]{:S(2)}, u32[]{:S(2)}) collective-permute-start(bf16[128,512]{1,0:T(8,128)(2,1)} %x_ref.5), channel_id=1, source_target_pairs={{0,1},{1,0},{2,3},{3,2},{4,5},{5,4},{6,7},{7,6},{8,9},{9,8},{10,11... | collective-permute-start | bytes 393224 | tf_op jit(solution)/shard_map/ppermute | solution.py:384
  15.1 3.1 %collective-permute-start.1 = (bf16[128,512]{1,0:T(8,128)(2,1)}, bf16[128,512]{1,0:T(8,128)(2,1)S(1)}, u32[]{:S(2)}, u32[]{:S(2)}) collective-permute-start(bf16[128,512]{1,0:T(8,128)(2,1)} %x_ref.5), channel_id=1, source_target_pairs={{1,2},{2,1},{3,4},{4,3},{5,6},{6,5},{7,8},{8,7},{9,10},{10,9},{11,... | collective-permute-start | bytes 393224 | tf_op jit(solution)/shard_map/ppermute | solution.py:384
  18.2 4.3 %all-to-all-done.1 = bf16[64,16,128]{2,1,0:T(8,128)(2,1)S(1)} async-done(((bf16[64,16,128]{2,1,0:T(8,128)(2,1)}), bf16[64,16,128]{2,1,0:T(8,128)(2,1)S(1)}, u32[]{:S(2)}, u32[]{:S(2)}) %all-to-all-start.1) | async-done | bytes 262176 | tf_op jit(solution)/shard_map/all_to_all | solution.py:408
  22.5 0.7 slice.12.refs_0_
  23.2 0.0 collective-permute-done.beside_ref
  23.2 0.0 collective-permute-done.1.across_ref
  23.2 10.0 %collective-permute-start.2 = (bf16[64,8,128]{2,1,0:T(8,128)(2,1)}, bf16[64,8,128]{2,1,0:T(8,128)(2,1)}, u32[]{:S(2)}, u32[]{:S(2)}) collective-permute-start(bf16[64,8,128]{2,1,0:T(8,128)(2,1)} %slice.12.refs_0_), channel_id=1, source_target_pairs={{0,64},{1,449},{64,128},{65,1},{128,192},{129,65},{192,256},{193,1... | collective-permute-start | bytes 393224 | tf_op jit(solution)/shard_map/ppermute | solution.py:371
  33.2 1.9 %collective-permute-start.6 = (bf16[64,8,128]{2,1,0:T(8,128)(2,1)}, bf16[64,8,128]{2,1,0:T(8,128)(2,1)}, u32[]{:S(2)}, u32[]{:S(2)}) collective-permute-start(bf16[64,8,128]{2,1,0:T(8,128)(2,1)} %slice.12.refs_0_), channel_id=1, source_target_pairs={{0,448},{1,65},{64,0},{65,129},{128,64},{129,193},{192,128},{193,2... | collective-permute-start | bytes 393224 | tf_op jit(solution)/shard_map/ppermute | solution.py:371
  35.1 1.5 %collective-permute-done.2.refs_1_ = bf16[64,8,128]{2,1,0:T(8,128)(2,1)} collective-permute-done((bf16[64,8,128]{2,1,0:T(8,128)(2,1)}, bf16[64,8,128]{2,1,0:T(8,128)(2,1)}, u32[]{:S(2)}, u32[]{:S(2)}) %collective-permute-start.2) | collective-permute-done | bytes 131104 | tf_op jit(solution)/shard_map/ppermute | solution.py:371
  36.6 5.9 %collective-permute-start.3 = (bf16[64,8,128]{2,1,0:T(8,128)(2,1)}, bf16[64,8,128]{2,1,0:T(8,128)(2,1)}, u32[]{:S(2)}, u32[]{:S(2)}) collective-permute-start(bf16[64,8,128]{2,1,0:T(8,128)(2,1)} %collective-permute-done.2.refs_1_), channel_id=1, source_target_pairs={{0,64},{1,449},{64,128},{65,1},{128,192},{129,65},{192,256},{193,1... | collective-permute-start | bytes 393224 | tf_op jit(solution)/shard_map/ppermute | solution.py:371
  42.5 0.0 collective-permute-done.6.refs_7_
  42.5 1.9 %collective-permute-start.7 = (bf16[64,8,128]{2,1,0:T(8,128)(2,1)}, bf16[64,8,128]{2,1,0:T(8,128)(2,1)}, u32[]{:S(2)}, u32[]{:S(2)}) collective-permute-start(bf16[64,8,128]{2,1,0:T(8,128)(2,1)} %collective-permute-done.6.refs_7_), channel_id=1, source_target_pairs={{0,448},{1,65},{64,0},{65,129},{128,64},{129,193},{192,128},{193,2... | collective-permute-start | bytes 393224 | tf_op jit(solution)/shard_map/ppermute | solution.py:371
  44.5 1.9 %collective-permute-done.3.refs_2_ = bf16[64,8,128]{2,1,0:T(8,128)(2,1)} collective-permute-done((bf16[64,8,128]{2,1,0:T(8,128)(2,1)}, bf16[64,8,128]{2,1,0:T(8,128)(2,1)}, u32[]{:S(2)}, u32[]{:S(2)}) %collective-permute-start.3) | collective-permute-done | bytes 131104 | tf_op jit(solution)/shard_map/ppermute | solution.py:371
  46.4 5.9 %collective-permute-start.4 = (bf16[64,8,128]{2,1,0:T(8,128)(2,1)}, bf16[64,8,128]{2,1,0:T(8,128)(2,1)}, u32[]{:S(2)}, u32[]{:S(2)}) collective-permute-start(bf16[64,8,128]{2,1,0:T(8,128)(2,1)} %collective-permute-done.3.refs_2_), channel_id=1, source_target_pairs={{0,64},{1,449},{64,128},{65,1},{128,192},{129,65},{192,256},{193,1... | collective-permute-start | bytes 393224 | tf_op jit(solution)/shard_map/ppermute | solution.py:371
  52.3 2.7 %collective-permute-done.7.refs_6_ = bf16[64,8,128]{2,1,0:T(8,128)(2,1)} collective-permute-done((bf16[64,8,128]{2,1,0:T(8,128)(2,1)}, bf16[64,8,128]{2,1,0:T(8,128)(2,1)}, u32[]{:S(2)}, u32[]{:S(2)}) %collective-permute-start.7) | collective-permute-done | bytes 131104 | tf_op jit(solution)/shard_map/ppermute | solution.py:371
  55.0 1.9 %collective-permute-start.8 = (bf16[64,8,128]{2,1,0:T(8,128)(2,1)}, bf16[64,8,128]{2,1,0:T(8,128)(2,1)}, u32[]{:S(2)}, u32[]{:S(2)}) collective-permute-start(bf16[64,8,128]{2,1,0:T(8,128)(2,1)} %collective-permute-done.7.refs_6_), channel_id=1, source_target_pairs={{0,448},{1,65},{64,0},{65,129},{128,64},{129,193},{192,128},{193,2... | collective-permute-start | bytes 393224 | tf_op jit(solution)/shard_map/ppermute | solution.py:371
  56.9 0.0 collective-permute-done.4.refs_3_
  56.9 0.1 reshape.182
  57.0 0.2 convert_reduce_fusion.1
  57.3 0.6 reshape.183
  57.9 0.1 broadcast_add_fusion
  57.9 0.6 add.129
  58.5 0.5 convert_reduce_fusion
  59.0 0.2 select_reduce_fusion
  59.3 5.5 %collective-permute-start.5 = (bf16[64,8,128]{2,1,0:T(8,128)(2,1)}, bf16[64,8,128]{2,1,0:T(8,128)(2,1)}, u32[]{:S(2)}, u32[]{:S(2)}) collective-permute-start(bf16[64,8,128]{2,1,0:T(8,128)(2,1)} %collective-permute-done.4.refs_3_), channel_id=1, source_target_pairs={{0,64},{1,449},{64,128},{65,1},{128,192},{129,65},{192,256},{193,1... | collective-permute-start | bytes 393224 | tf_op jit(solution)/shard_map/ppermute | solution.py:371
  64.7 0.6 minimum_add_fusion.1.at_ref
  65.4 0.0 collective-permute-done.8.refs_5_
  65.4 3.3 %collective-permute-done.5.refs_4_ = bf16[64,8,128]{2,1,0:T(8,128)(2,1)} collective-permute-done((bf16[64,8,128]{2,1,0:T(8,128)(2,1)}, bf16[64,8,128]{2,1,0:T(8,128)(2,1)}, u32[]{:S(2)}, u32[]{:S(2)}) %collective-permute-start.5) | collective-permute-done | bytes 131104 | tf_op jit(solution)/shard_map/ppermute | solution.py:371
  68.6 3.7 %select.78 = bf16[64,15,8,128]{3,2,1,0:T(8,128)(2,1)} custom-call(s32[64]{0:T(128)S(1)} %minimum_add_fusion.1.at_ref, s32[1039]{0:T(1024)S(1)} %concatenate.6.list_ref, bf16[64,8,128]{2,1,0:T(8,128)(2,1)} %slice.12.refs_0_, bf16[64,8,128]{2,1,0:T(8,128)(2,1)} %collective-permute-done.2.refs_1_, bf16[64,8,128]{2,1,0:T(8,128)(2,1)} %collective-permute-done.3.refs_2_, ...), custom_call_target="tpu_custom_call" | custom-call | bytes 8388608 | tf_op jit(solution)/shard_map/select/pallas_call | solution.py:180
  72.4 0.0 copy-start.3
  72.4 0.0 copy-start
  72.4 0.0 copy-start.1
  72.4 0.0 copy-start.2
  72.4 0.0 copy-start.4
  72.4 13.6 %all-to-all-start.2 = ((bf16[64,15,8,128]{3,2,1,0:T(8,128)(2,1)}), bf16[64,15,8,128]{3,2,1,0:T(8,128)(2,1)}, u32[]{:S(2)}, u32[]{:S(2)}) async-start(bf16[64,15,8,128]{3,2,1,0:T(8,128)(2,1)} %select.78), calls=%async_computation.2 | async-start | bytes 3932160 | tf_op jit(solution)/shard_map/all_to_all | solution.py:408
  86.1 0.0 copy-done.3
  86.1 0.1 fusion.8
  86.2 0.1 bitcast_select_fusion
  86.3 0.1 broadcast_in_dim.71.kid_ref
  86.4 0.0 copy-start.6
  86.4 0.0 copy-start.8
  86.4 0.0 copy-start.10
  86.4 0.0 copy-start.12
  86.5 0.0 copy-start.14
  86.5 0.0 copy-start.16
  86.5 0.1 fusion.3
  86.6 0.0 copy-done
  86.6 0.0 copy-done.1
  86.6 0.0 copy-done.2
  86.6 0.0 copy-done.4
  86.6 2.1 %near.1 = (bf16[4,128,256]{2,1,0:T(8,128)(2,1)S(1)}, f32[4,256]{1,0:T(4,128)S(1)}, f32[4,256]{1,0:T(4,128)S(1)}, f32[512,128]{1,0:T(8,128)S(1)}) custom-call(bf16[128,512]{1,0:T(8,128)(2,1)S(1)} %collective-permute-done.beside_ref, bf16[128,512]{1,0:T(8,128)(2,1)S(1)} %copy-done.4, bf16[128,512]{1,0:T(8,128)(2,1)S(1)} %collective-permute-done.1.across_ref, ...), custom_call_target="tpu_custom_call" | custom-call | flops 1000000000 | bytes 3145728 | tf_op jit(solution)/shard_map/near/pallas_call | solution.py:134
  88.7 1.2 dynamic_slice.11
  89.9 0.7 reduce_max.9
  92.0 21.7 %all-to-all-done.2.held_ref = bf16[64,15,8,128]{3,2,1,0:T(8,128)(2,1)} async-done(((bf16[64,15,8,128]{3,2,1,0:T(8,128)(2,1)}), bf16[64,15,8,128]{3,2,1,0:T(8,128)(2,1)}, u32[]{:S(2)}, u32[]{:S(2)}) %all-to-all-start.2) | async-done | bytes 1966112 | tf_op jit(solution)/shard_map/all_to_all | solution.py:408
  113.7 0.0 copy-done.6
  113.7 0.0 copy-done.8
  113.7 0.0 copy-done.10
  113.7 0.0 copy-done.12
  113.7 0.0 copy-done.14
  113.7 0.0 copy-done.16
  113.7 8.4 %finish.3 = (f32[128,512]{1,0:T(8,128)}, f32[4,256]{1,0:T(4,128)S(1)}, f32[4,256]{1,0:T(4,128)S(1)}, f32[512,128]{1,0:T(8,128)S(1)}) custom-call(s32[1]{0:T(128)S(6)} %min.29.count_ref, bf16[64,15,8,128]{3,2,1,0:T(8,128)(2,1)} %all-to-all-done.2.held_ref, bf16[4,128,256]{2,1,0:T(8,128)(2,1)S(1)} %get-tuple-element.341.query_ref, ...), custom_call_target="tpu_custom_call" | custom-call | flops 4000000000 | bytes 8388608 | tf_op jit(solution)/shard_map/finish/pallas_call | solution.py:307
  122.1 0.2 conditional.1
  (11 shorter events, 0.1 us)
Async XLA Ops:
  1.6 20.9 %all-to-all-start.1 = ((bf16[64,16,128]{2,1,0:T(8,128)(2,1)}), bf16[64,16,128]{2,1,0:T(8,128)(2,1)S(1)}, u32[]{:S(2)}, u32[]{:S(2)}) async-start(bf16[64,16,128]{2,1,0:T(8,128)(2,1)} %pack.1), calls=%async_computation.1 | async-start | bytes 524288 | tf_op jit(solution)/shard_map/all_to_all | solution.py:408
  12.6 10.6 %collective-permute-start = (bf16[128,512]{1,0:T(8,128)(2,1)}, bf16[128,512]{1,0:T(8,128)(2,1)S(1)}, u32[]{:S(2)}, u32[]{:S(2)}) collective-permute-start(bf16[128,512]{1,0:T(8,128)(2,1)} %x_ref.5), channel_id=1, source_target_pairs={{0,1},{1,0},{2,3},{3,2},{4,5},{5,4},{6,7},{7,6},{8,9},{9,8},{10,11... | collective-permute-start | bytes 393224 | tf_op jit(solution)/shard_map/ppermute | solution.py:384
  15.1 8.1 %collective-permute-start.1 = (bf16[128,512]{1,0:T(8,128)(2,1)}, bf16[128,512]{1,0:T(8,128)(2,1)S(1)}, u32[]{:S(2)}, u32[]{:S(2)}) collective-permute-start(bf16[128,512]{1,0:T(8,128)(2,1)} %x_ref.5), channel_id=1, source_target_pairs={{1,2},{2,1},{3,4},{4,3},{5,6},{6,5},{7,8},{8,7},{9,10},{10,9},{11,... | collective-permute-start | bytes 393224 | tf_op jit(solution)/shard_map/ppermute | solution.py:384
  23.2 13.4 %collective-permute-start.2 = (bf16[64,8,128]{2,1,0:T(8,128)(2,1)}, bf16[64,8,128]{2,1,0:T(8,128)(2,1)}, u32[]{:S(2)}, u32[]{:S(2)}) collective-permute-start(bf16[64,8,128]{2,1,0:T(8,128)(2,1)} %slice.12.refs_0_), channel_id=1, source_target_pairs={{0,64},{1,449},{64,128},{65,1},{128,192},{129,65},{192,256},{193,1... | collective-permute-start | bytes 393224 | tf_op jit(solution)/shard_map/ppermute | solution.py:371
  33.2 9.4 %collective-permute-start.6 = (bf16[64,8,128]{2,1,0:T(8,128)(2,1)}, bf16[64,8,128]{2,1,0:T(8,128)(2,1)}, u32[]{:S(2)}, u32[]{:S(2)}) collective-permute-start(bf16[64,8,128]{2,1,0:T(8,128)(2,1)} %slice.12.refs_0_), channel_id=1, source_target_pairs={{0,448},{1,65},{64,0},{65,129},{128,64},{129,193},{192,128},{193,2... | collective-permute-start | bytes 393224 | tf_op jit(solution)/shard_map/ppermute | solution.py:371
  36.6 9.8 %collective-permute-start.3 = (bf16[64,8,128]{2,1,0:T(8,128)(2,1)}, bf16[64,8,128]{2,1,0:T(8,128)(2,1)}, u32[]{:S(2)}, u32[]{:S(2)}) collective-permute-start(bf16[64,8,128]{2,1,0:T(8,128)(2,1)} %collective-permute-done.2.refs_1_), channel_id=1, source_target_pairs={{0,64},{1,449},{64,128},{65,1},{128,192},{129,65},{192,256},{193,1... | collective-permute-start | bytes 393224 | tf_op jit(solution)/shard_map/ppermute | solution.py:371
  42.5 12.5 %collective-permute-start.7 = (bf16[64,8,128]{2,1,0:T(8,128)(2,1)}, bf16[64,8,128]{2,1,0:T(8,128)(2,1)}, u32[]{:S(2)}, u32[]{:S(2)}) collective-permute-start(bf16[64,8,128]{2,1,0:T(8,128)(2,1)} %collective-permute-done.6.refs_7_), channel_id=1, source_target_pairs={{0,448},{1,65},{64,0},{65,129},{128,64},{129,193},{192,128},{193,2... | collective-permute-start | bytes 393224 | tf_op jit(solution)/shard_map/ppermute | solution.py:371
  46.4 10.5 %collective-permute-start.4 = (bf16[64,8,128]{2,1,0:T(8,128)(2,1)}, bf16[64,8,128]{2,1,0:T(8,128)(2,1)}, u32[]{:S(2)}, u32[]{:S(2)}) collective-permute-start(bf16[64,8,128]{2,1,0:T(8,128)(2,1)} %collective-permute-done.3.refs_2_), channel_id=1, source_target_pairs={{0,64},{1,449},{64,128},{65,1},{128,192},{129,65},{192,256},{193,1... | collective-permute-start | bytes 393224 | tf_op jit(solution)/shard_map/ppermute | solution.py:371
  55.0 10.4 %collective-permute-start.8 = (bf16[64,8,128]{2,1,0:T(8,128)(2,1)}, bf16[64,8,128]{2,1,0:T(8,128)(2,1)}, u32[]{:S(2)}, u32[]{:S(2)}) collective-permute-start(bf16[64,8,128]{2,1,0:T(8,128)(2,1)} %collective-permute-done.7.refs_6_), channel_id=1, source_target_pairs={{0,448},{1,65},{64,0},{65,129},{128,64},{129,193},{192,128},{193,2... | collective-permute-start | bytes 393224 | tf_op jit(solution)/shard_map/ppermute | solution.py:371
  59.3 9.4 %collective-permute-start.5 = (bf16[64,8,128]{2,1,0:T(8,128)(2,1)}, bf16[64,8,128]{2,1,0:T(8,128)(2,1)}, u32[]{:S(2)}, u32[]{:S(2)}) collective-permute-start(bf16[64,8,128]{2,1,0:T(8,128)(2,1)} %collective-permute-done.4.refs_3_), channel_id=1, source_target_pairs={{0,64},{1,449},{64,128},{65,1},{128,192},{129,65},{192,256},{193,1... | collective-permute-start | bytes 393224 | tf_op jit(solution)/shard_map/ppermute | solution.py:371
  72.4 13.7 %copy-start.3 = (s32[65536]{0:T(1024)S(1)}, s32[65536]{0:T(1024)}, u32[]{:S(2)}) copy-start(s32[65536]{0:T(1024)} %param.20) | copy-start | bytes 786436
  72.4 14.2 %copy-start = (bf16[512,512]{1,0:T(8,128)(2,1)S(1)}, bf16[512,512]{1,0:T(8,128)(2,1)}, u32[]{:S(2)}) copy-start(bf16[512,512]{1,0:T(8,128)(2,1)} %wq_ref.1) | copy-start | bytes 1572868
  72.4 14.2 %copy-start.1 = (bf16[512,512]{1,0:T(8,128)(2,1)S(1)}, bf16[512,512]{1,0:T(8,128)(2,1)}, u32[]{:S(2)}) copy-start(bf16[512,512]{1,0:T(8,128)(2,1)} %wk_ref.3) | copy-start | bytes 1572868
  72.4 14.2 %copy-start.2 = (bf16[512,512]{1,0:T(8,128)(2,1)S(1)}, bf16[512,512]{1,0:T(8,128)(2,1)}, u32[]{:S(2)}) copy-start(bf16[512,512]{1,0:T(8,128)(2,1)} %wv_ref.3) | copy-start | bytes 1572868
  72.4 14.2 %copy-start.4 = (bf16[128,512]{1,0:T(8,128)(2,1)S(1)}, bf16[128,512]{1,0:T(8,128)(2,1)}, u32[]{:S(2)}) copy-start(bf16[128,512]{1,0:T(8,128)(2,1)} %x_ref.5) | copy-start | bytes 393220
  72.4 41.2 %all-to-all-start.2 = ((bf16[64,15,8,128]{3,2,1,0:T(8,128)(2,1)}), bf16[64,15,8,128]{3,2,1,0:T(8,128)(2,1)}, u32[]{:S(2)}, u32[]{:S(2)}) async-start(bf16[64,15,8,128]{3,2,1,0:T(8,128)(2,1)} %select.78), calls=%async_computation.2 | async-start | bytes 3932160 | tf_op jit(solution)/shard_map/all_to_all | solution.py:408
  86.4 27.3 %copy-start.6 = (bf16[512,512]{1,0:T(8,128)(2,1)S(1)}, bf16[512,512]{1,0:T(8,128)(2,1)}, u32[]{:S(2)}) copy-start(bf16[512,512]{1,0:T(8,128)(2,1)} %w_out_hbm.1) | copy-start | bytes 1572868
  86.4 27.3 %copy-start.8 = (f32[1024]{0:T(1024)S(1)}, f32[1024]{0:T(1024)}, u32[]{:S(2)}) copy-start(f32[1024]{0:T(1024)} %param.30) | copy-start | bytes 12292
  86.4 27.2 %copy-start.10 = (f32[512]{0:T(512)S(1)}, f32[512]{0:T(512)}, u32[]{:S(2)}) copy-start(f32[512]{0:T(512)} %param.27) | copy-start | bytes 6148
  86.4 27.2 %copy-start.12 = (f32[512]{0:T(512)S(1)}, f32[512]{0:T(512)}, u32[]{:S(2)}) copy-start(f32[512]{0:T(512)} %param.28) | copy-start | bytes 6148
  86.5 27.2 %copy-start.14 = (f32[512]{0:T(512)S(1)}, f32[512]{0:T(512)}, u32[]{:S(2)}) copy-start(f32[512]{0:T(512)} %param.32) | copy-start | bytes 6148
  86.5 27.2 %copy-start.16 = (f32[512]{0:T(512)S(1)}, f32[512]{0:T(512)}, u32[]{:S(2)}) copy-start(f32[512]{0:T(512)} %param.33) | copy-start | bytes 6148

commit v2 on v0

--- a/solution.py
+++ b/solution.py
@@ -160,7 +160,7 @@
     )(x, pair_tiles[0].T, pair_count)
 
 
-def select_kernel(at_ref, list_ref, *refs):
+def select_kernel(at_ref, start_ref, count_ref, list_ref, *refs):
     sources, out_ref, all_ref = refs[:-2], refs[-2], refs[-1]
     at = 0
     for source in sources:
@@ -168,25 +168,26 @@
         at += source.shape[0]
 
     def one(dest, carry):
-        at = at_ref[dest]
+        group, member = dest // MEMBERS, dest % MEMBERS
+        at = start_ref[group, member] + jnp.minimum(at_ref[0], count_ref[group, member])
         for slot in range(SLOTS):
-            out_ref[dest, slot] = all_ref[list_ref[at + slot]]
+            out_ref[dest, slot] = all_ref[list_ref[group, at + slot]]
         return carry
 
     lax.fori_loop(0, SLAB_BLOCKS, one, 0, unroll=4)
 
 
-def select(at, pairs, gathered):
+def select(at, start, count, pairs, gathered):
     return pl.pallas_call(
         select_kernel,
-        in_specs=[SMEM] * 2 + [VMEM] * len(gathered),
+        in_specs=[SMEM] * 4 + [VMEM] * len(gathered),
         out_specs=VMEM,
         out_shape=jax.ShapeDtypeStruct((SLAB_BLOCKS, SLOTS, TILE_ROWS, TILE_COLS), BF16),
         scratch_shapes=[pltpu.VMEM((sum(g.shape[0] for g in gathered), TILE_ROWS, TILE_COLS), BF16)],
         compiler_params=pltpu.CompilerParams(vmem_limit_bytes=32 * MIB),
         cost_estimate=pl.CostEstimate(flops=0, bytes_accessed=8 * MIB, transcendentals=0),
         name="select",
-    )(at, pairs, *gathered)
+    )(at, start, count, pairs, *gathered)
 
 
 def gather_block(held_ref, slot):
@@ -351,12 +352,11 @@
     )
     place = jnp.sum(ahead.astype(jnp.int32), axis=-1)
     pairs = jnp.sum(jnp.where(place[:, None, :] == slot[None, :, None], key_slot[:, None, :], 0), axis=-1)
-    pairs = jnp.concatenate([pairs.reshape(-1), jnp.zeros((SLOTS,), jnp.int32)])
+    pairs = jnp.pad(pairs, ((0, 0), (0, SLOTS)))
     member = jnp.arange(MEMBERS, dtype=jnp.int32)[None, :, None]
     start = jnp.sum((query_index[:, None, :] < member).astype(jnp.int32), axis=-1)
     count = jnp.sum((query_index[:, None, :] == member).astype(jnp.int32), axis=-1)
-    start = start + size * jnp.arange(SLAB_GROUPS, dtype=jnp.int32)[:, None]
-    return start.reshape(-1), count.reshape(-1), pairs
+    return start, count, pairs
 
 
 def gather_rings(tiles):
@@ -415,7 +415,7 @@
     start, count, pairs = pair_lists(codes.reshape(SLAB_GROUPS, -1), z_high, core)
 
     def mine(value):
-        return lax.dynamic_slice_in_dim(value, own, 1, 0)
+        return lax.dynamic_slice_in_dim(value.reshape(-1), own, 1, 0)
 
     fill = jnp.full((ROWS,), -1, jnp.int32)
     ids = jnp.concatenate([fill, graph_ids, fill])
@@ -428,7 +428,7 @@
     )
 
     def fetch(at):
-        held = exchange(select(start + jnp.minimum(at, count), pairs, gathered))
+        held = exchange(select(at.reshape(1), start, count, pairs, gathered))
         return jnp.clip(mine(count) - at, 0, SLOTS), held
 
     def close(part, held, state):

time: 120 us -> 123 us (1.025)
  Pallas kernels: 13.5 us -> 18 us
  local copies, waits for them, and re-layouts: 3.41 us -> 1.66 us
    pallas_call x1, Pallas kernels: 5.99 us -> 8.39 us  [finish(): pl.pallas_call(finish_kernel, in_specs=[SMEM] + [VMEM] * 13 + [hbm] * 3,...]
    pallas_call x1, Pallas kernels: 3.75 us -> 5.87 us  [select(): pl.pallas_call(select_kernel, in_specs=[SMEM] * 4 + [VMEM] * len(gathered...]
  transfers between devices with their start and end apart: 11 -> 11, of which waited for: 7 -> 7; matrix products, arithmetic and copies ran while one was open for 5% -> 3% of each run, Pallas kernels for 2% -> 2%
where the time goes in v2:
time: 123 us; the launch traced here: 122 us
  starting transfers between devices  61.6 us (50%)
  waiting for transfers between devices  36.5 us (30%)
  Pallas kernels  18 us (15%)
  other arithmetic  2.45 us (2%)
  between operations  1.83 us (1%)
  local copies, waits for them, and re-layouts  1.66 us (1%)
    ppermute x7, starting transfers between devices, move(): return lax.ppermute(value, ('zhi', 'core'), pairs)  33 us
    all_to_all x2, waiting for transfers between devices, exchange(): return lax.all_to_all(value, SLAB, split_axis=0, concat_axis=0, tiled=True)  26.5 us
    all_to_all x2, starting transfers between devices, exchange(): return lax.all_to_all(value, SLAB, split_axis=0, concat_axis=0, tiled=True)  23 us
    ppermute x7, waiting for transfers between devices, move(): return lax.ppermute(value, ('zhi', 'core'), pairs)  9.98 us
    pallas_call x1, Pallas kernels, finish(): pl.pallas_call(finish_kernel, in_specs=[SMEM] + [VMEM] * 13 + [hbm] * 3,...  8.39 us
    pallas_call x1, Pallas kernels, select(): pl.pallas_call(select_kernel, in_specs=[SMEM] * 4 + [VMEM] * len(gathered...  5.87 us
    ppermute x2, starting transfers between devices, swap(): lax.ppermute(x, AXES, [p for a, b in pairs for p in ((a, b), (b, a))])  5.61 us
  transfers between devices with their start and end apart: 11, of which 7 were waited for; matrix products, arithmetic and copies ran while one was open for 3% of the time, Pallas kernels for 2%

profile of v2, /device:TPU:1, one launch (start us, length us, event | category | flops | bytes accessed | tf_op | source)
XLA Modules:
  0.0 122.3 jit_solution(15013295849724095349)
XLA Ops:
  0.0 1.6 %pack.1 = bf16[64,16,128]{2,1,0:T(8,128)(2,1)} custom-call(bf16[128,512]{1,0:T(8,128)(2,1)} %x_ref.5, s32[8,32]{1,0:T(8,128)} %bitcast.22, s32[1,32]{1,0:T(1,128)} %counts_ref.1), custom_call_target="tpu_custom_call" | custom-call | tf_op jit(solution)/shard_map/pack/pallas_call | solution.py:155
  1.6 10.9 %all-to-all-start.1 = ((bf16[64,16,128]{2,1,0:T(8,128)(2,1)}), bf16[64,16,128]{2,1,0:T(8,128)(2,1)S(1)}, u32[]{:S(2)}, u32[]{:S(2)}) async-start(bf16[64,16,128]{2,1,0:T(8,128)(2,1)} %pack.1), calls=%async_computation.1 | async-start | bytes 524288 | tf_op jit(solution)/shard_map/all_to_all | solution.py:406
  12.6 2.5 %collective-permute-start = (bf16[128,512]{1,0:T(8,128)(2,1)}, bf16[128,512]{1,0:T(8,128)(2,1)S(1)}, u32[]{:S(2)}, u32[]{:S(2)}) collective-permute-start(bf16[128,512]{1,0:T(8,128)(2,1)} %x_ref.5), channel_id=1, source_target_pairs={{0,1},{1,0},{2,3},{3,2},{4,5},{5,4},{6,7},{7,6},{8,9},{9,8},{10,11... | collective-permute-start | bytes 393224 | tf_op jit(solution)/shard_map/ppermute | solution.py:382
  15.1 3.1 %collective-permute-start.1 = (bf16[128,512]{1,0:T(8,128)(2,1)}, bf16[128,512]{1,0:T(8,128)(2,1)S(1)}, u32[]{:S(2)}, u32[]{:S(2)}) collective-permute-start(bf16[128,512]{1,0:T(8,128)(2,1)} %x_ref.5), channel_id=1, source_target_pairs={{1,2},{2,1},{3,4},{4,3},{5,6},{6,5},{7,8},{8,7},{9,10},{10,9},{11,... | collective-permute-start | bytes 393224 | tf_op jit(solution)/shard_map/ppermute | solution.py:382
  18.3 4.2 %all-to-all-done.1 = bf16[64,16,128]{2,1,0:T(8,128)(2,1)S(1)} async-done(((bf16[64,16,128]{2,1,0:T(8,128)(2,1)}), bf16[64,16,128]{2,1,0:T(8,128)(2,1)S(1)}, u32[]{:S(2)}, u32[]{:S(2)}) %all-to-all-start.1) | async-done | bytes 262176 | tf_op jit(solution)/shard_map/all_to_all | solution.py:406
  22.5 0.7 slice.12.refs_0_
  23.2 0.0 collective-permute-done.beside_ref
  23.2 0.0 collective-permute-done.1.across_ref
  23.2 10.0 %collective-permute-start.2 = (bf16[64,8,128]{2,1,0:T(8,128)(2,1)}, bf16[64,8,128]{2,1,0:T(8,128)(2,1)}, u32[]{:S(2)}, u32[]{:S(2)}) collective-permute-start(bf16[64,8,128]{2,1,0:T(8,128)(2,1)} %slice.12.refs_0_), channel_id=1, source_target_pairs={{0,64},{1,449},{64,128},{65,1},{128,192},{129,65},{192,256},{193,1... | collective-permute-start | bytes 393224 | tf_op jit(solution)/shard_map/ppermute | solution.py:371
  33.2 1.9 %collective-permute-start.6 = (bf16[64,8,128]{2,1,0:T(8,128)(2,1)}, bf16[64,8,128]{2,1,0:T(8,128)(2,1)}, u32[]{:S(2)}, u32[]{:S(2)}) collective-permute-start(bf16[64,8,128]{2,1,0:T(8,128)(2,1)} %slice.12.refs_0_), channel_id=1, source_target_pairs={{0,448},{1,65},{64,0},{65,129},{128,64},{129,193},{192,128},{193,2... | collective-permute-start | bytes 393224 | tf_op jit(solution)/shard_map/ppermute | solution.py:371
  35.1 0.1 reshape.185
  35.2 1.4 %collective-permute-done.2.refs_1_ = bf16[64,8,128]{2,1,0:T(8,128)(2,1)} collective-permute-done((bf16[64,8,128]{2,1,0:T(8,128)(2,1)}, bf16[64,8,128]{2,1,0:T(8,128)(2,1)}, u32[]{:S(2)}, u32[]{:S(2)}) %collective-permute-start.2) | collective-permute-done | bytes 131104 | tf_op jit(solution)/shard_map/ppermute | solution.py:371
  36.6 5.9 %collective-permute-start.3 = (bf16[64,8,128]{2,1,0:T(8,128)(2,1)}, bf16[64,8,128]{2,1,0:T(8,128)(2,1)}, u32[]{:S(2)}, u32[]{:S(2)}) collective-permute-start(bf16[64,8,128]{2,1,0:T(8,128)(2,1)} %collective-permute-done.2.refs_1_), channel_id=1, source_target_pairs={{0,64},{1,449},{64,128},{65,1},{128,192},{129,65},{192,256},{193,1... | collective-permute-start | bytes 393224 | tf_op jit(solution)/shard_map/ppermute | solution.py:371
  42.5 0.0 collective-permute-done.6.refs_7_
  42.5 1.9 %collective-permute-start.7 = (bf16[64,8,128]{2,1,0:T(8,128)(2,1)}, bf16[64,8,128]{2,1,0:T(8,128)(2,1)}, u32[]{:S(2)}, u32[]{:S(2)}) collective-permute-start(bf16[64,8,128]{2,1,0:T(8,128)(2,1)} %collective-permute-done.6.refs_7_), channel_id=1, source_target_pairs={{0,448},{1,65},{64,0},{65,129},{128,64},{129,193},{192,128},{193,2... | collective-permute-start | bytes 393224 | tf_op jit(solution)/shard_map/ppermute | solution.py:371
  44.5 1.9 %collective-permute-done.3.refs_2_ = bf16[64,8,128]{2,1,0:T(8,128)(2,1)} collective-permute-done((bf16[64,8,128]{2,1,0:T(8,128)(2,1)}, bf16[64,8,128]{2,1,0:T(8,128)(2,1)}, u32[]{:S(2)}, u32[]{:S(2)}) %collective-permute-start.3) | collective-permute-done | bytes 131104 | tf_op jit(solution)/shard_map/ppermute | solution.py:371
  46.4 5.9 %collective-permute-start.4 = (bf16[64,8,128]{2,1,0:T(8,128)(2,1)}, bf16[64,8,128]{2,1,0:T(8,128)(2,1)}, u32[]{:S(2)}, u32[]{:S(2)}) collective-permute-start(bf16[64,8,128]{2,1,0:T(8,128)(2,1)} %collective-permute-done.3.refs_2_), channel_id=1, source_target_pairs={{0,64},{1,449},{64,128},{65,1},{128,192},{129,65},{192,256},{193,1... | collective-permute-start | bytes 393224 | tf_op jit(solution)/shard_map/ppermute | solution.py:371
  52.3 0.5 convert_reduce_fusion
  52.8 2.2 %collective-permute-done.7.refs_6_ = bf16[64,8,128]{2,1,0:T(8,128)(2,1)} collective-permute-done((bf16[64,8,128]{2,1,0:T(8,128)(2,1)}, bf16[64,8,128]{2,1,0:T(8,128)(2,1)}, u32[]{:S(2)}, u32[]{:S(2)}) %collective-permute-start.7) | collective-permute-done | bytes 131104 | tf_op jit(solution)/shard_map/ppermute | solution.py:371
  55.0 1.9 %collective-permute-start.8 = (bf16[64,8,128]{2,1,0:T(8,128)(2,1)}, bf16[64,8,128]{2,1,0:T(8,128)(2,1)}, u32[]{:S(2)}, u32[]{:S(2)}) collective-permute-start(bf16[64,8,128]{2,1,0:T(8,128)(2,1)} %collective-permute-done.7.refs_6_), channel_id=1, source_target_pairs={{0,448},{1,65},{64,0},{65,129},{128,64},{129,193},{192,128},{193,2... | collective-permute-start | bytes 393224 | tf_op jit(solution)/shard_map/ppermute | solution.py:371
  56.9 0.0 collective-permute-done.4.refs_3_
  56.9 5.5 %collective-permute-start.5 = (bf16[64,8,128]{2,1,0:T(8,128)(2,1)}, bf16[64,8,128]{2,1,0:T(8,128)(2,1)}, u32[]{:S(2)}, u32[]{:S(2)}) collective-permute-start(bf16[64,8,128]{2,1,0:T(8,128)(2,1)} %collective-permute-done.4.refs_3_), channel_id=1, source_target_pairs={{0,64},{1,449},{64,128},{65,1},{128,192},{129,65},{192,256},{193,1... | collective-permute-start | bytes 393224 | tf_op jit(solution)/shard_map/ppermute | solution.py:371
  62.4 0.2 select_reduce_fusion
  62.6 0.7 convert_reduce_fusion.1
  63.4 0.6 collective-permute-done.8.refs_5_
  64.0 3.8 %collective-permute-done.5.refs_4_ = bf16[64,8,128]{2,1,0:T(8,128)(2,1)} collective-permute-done((bf16[64,8,128]{2,1,0:T(8,128)(2,1)}, bf16[64,8,128]{2,1,0:T(8,128)(2,1)}, u32[]{:S(2)}, u32[]{:S(2)}) %collective-permute-start.5) | collective-permute-done | bytes 131104 | tf_op jit(solution)/shard_map/ppermute | solution.py:371
  67.8 5.9 %select.78 = bf16[64,15,8,128]{3,2,1,0:T(8,128)(2,1)} custom-call(s32[1]{0:T(128)} %constant.124.clone.1.at_ref, s32[4,16]{1,0:T(4,128)} %get-tuple-element.343.start_ref, s32[4,16]{1,0:T(4,128)S(1)} %get-tuple-element.344.count_ref, s32[4,271]{1,0:T(4,128)S(1)} %pad.4.list_ref, bf16[64,8,128]{2,1,0:T(8,128)(2,1)} %slice.12.refs_0_, ...), custom_call_target="tpu_custom_call" | custom-call | bytes 8388608 | tf_op jit(solution)/shard_map/select/pallas_call | solution.py:181
  73.7 0.0 copy-start.4
  73.7 0.0 copy-start.1
  73.7 0.0 copy-start.2
  73.7 0.0 copy-start.3
  73.7 0.0 copy-start.5
  73.7 12.1 %all-to-all-start.2 = ((bf16[64,15,8,128]{3,2,1,0:T(8,128)(2,1)}), bf16[64,15,8,128]{3,2,1,0:T(8,128)(2,1)}, u32[]{:S(2)}, u32[]{:S(2)}) async-start(bf16[64,15,8,128]{3,2,1,0:T(8,128)(2,1)} %select.78), calls=%async_computation.2 | async-start | bytes 3932160 | tf_op jit(solution)/shard_map/all_to_all | solution.py:406
  85.9 0.0 copy-done.4
  85.9 0.1 fusion.8
  86.0 0.1 bitcast_select_fusion
  86.1 0.1 broadcast_in_dim.70.kid_ref
  86.2 0.0 copy-start.7
  86.2 0.0 copy-start.9
  86.2 0.0 copy-start.11
  86.2 0.0 copy-start.13
  86.2 0.0 copy-start.15
  86.3 0.0 copy-start.17
  86.3 0.1 fusion.3
  86.4 0.1 reshape.181
  86.5 0.6 dynamic_slice.11
  87.7 0.7 reduce_max.9
  89.0 0.0 copy-done.1
  89.0 0.0 copy-done.2
  89.0 0.0 copy-done.3
  89.0 0.0 copy-done.5
  89.1 2.1 %near.1 = (bf16[4,128,256]{2,1,0:T(8,128)(2,1)S(1)}, f32[4,256]{1,0:T(4,128)S(1)}, f32[4,256]{1,0:T(4,128)S(1)}, f32[512,128]{1,0:T(8,128)S(1)}) custom-call(bf16[128,512]{1,0:T(8,128)(2,1)S(1)} %collective-permute-done.beside_ref, bf16[128,512]{1,0:T(8,128)(2,1)S(1)} %copy-done.5, bf16[128,512]{1,0:T(8,128)(2,1)S(1)} %collective-permute-done.1.across_ref, ...), custom_call_target="tpu_custom_call" | custom-call | flops 1000000000 | bytes 3145728 | tf_op jit(solution)/shard_map/near/pallas_call | solution.py:134
  91.2 22.3 %all-to-all-done.2.held_ref = bf16[64,15,8,128]{3,2,1,0:T(8,128)(2,1)} async-done(((bf16[64,15,8,128]{3,2,1,0:T(8,128)(2,1)}), bf16[64,15,8,128]{3,2,1,0:T(8,128)(2,1)}, u32[]{:S(2)}, u32[]{:S(2)}) %all-to-all-start.2) | async-done | bytes 1966112 | tf_op jit(solution)/shard_map/all_to_all | solution.py:406
  113.5 0.0 copy-done.7
  113.5 0.0 copy-done.9
  113.5 0.0 copy-done.11
  113.5 0.0 copy-done.13
  113.5 0.0 copy-done.15
  113.5 0.0 copy-done.17
  113.5 8.4 %finish.3 = (f32[128,512]{1,0:T(8,128)}, f32[4,256]{1,0:T(4,128)S(1)}, f32[4,256]{1,0:T(4,128)}, f32[512,128]{1,0:T(8,128)S(1)}) custom-call(s32[1]{0:T(128)S(6)} %min.13.count_ref, bf16[64,15,8,128]{3,2,1,0:T(8,128)(2,1)} %all-to-all-done.2.held_ref, bf16[4,128,256]{2,1,0:T(8,128)(2,1)S(1)} %get-tuple-element.334.query_ref, bf16[512,512]{1,0:T(8,128)(2,1)S(1)} %copy-done.2, ...), custom_call_target="tpu_custom_call" | custom-call | flops 4000000000 | bytes 8388608 | tf_op jit(solution)/shard_map/finish/pallas_call | solution.py:308
  121.9 0.2 conditional.1
  (9 shorter events, 0.1 us)
Async XLA Ops:
  1.6 20.9 %all-to-all-start.1 = ((bf16[64,16,128]{2,1,0:T(8,128)(2,1)}), bf16[64,16,128]{2,1,0:T(8,128)(2,1)S(1)}, u32[]{:S(2)}, u32[]{:S(2)}) async-start(bf16[64,16,128]{2,1,0:T(8,128)(2,1)} %pack.1), calls=%async_computation.1 | async-start | bytes 524288 | tf_op jit(solution)/shard_map/all_to_all | solution.py:406
  12.6 10.6 %collective-permute-start = (bf16[128,512]{1,0:T(8,128)(2,1)}, bf16[128,512]{1,0:T(8,128)(2,1)S(1)}, u32[]{:S(2)}, u32[]{:S(2)}) collective-permute-start(bf16[128,512]{1,0:T(8,128)(2,1)} %x_ref.5), channel_id=1, source_target_pairs={{0,1},{1,0},{2,3},{3,2},{4,5},{5,4},{6,7},{7,6},{8,9},{9,8},{10,11... | collective-permute-start | bytes 393224 | tf_op jit(solution)/shard_map/ppermute | solution.py:382
  15.1 8.1 %collective-permute-start.1 = (bf16[128,512]{1,0:T(8,128)(2,1)}, bf16[128,512]{1,0:T(8,128)(2,1)S(1)}, u32[]{:S(2)}, u32[]{:S(2)}) collective-permute-start(bf16[128,512]{1,0:T(8,128)(2,1)} %x_ref.5), channel_id=1, source_target_pairs={{1,2},{2,1},{3,4},{4,3},{5,6},{6,5},{7,8},{8,7},{9,10},{10,9},{11,... | collective-permute-start | bytes 393224 | tf_op jit(solution)/shard_map/ppermute | solution.py:382
  23.2 13.4 %collective-permute-start.2 = (bf16[64,8,128]{2,1,0:T(8,128)(2,1)}, bf16[64,8,128]{2,1,0:T(8,128)(2,1)}, u32[]{:S(2)}, u32[]{:S(2)}) collective-permute-start(bf16[64,8,128]{2,1,0:T(8,128)(2,1)} %slice.12.refs_0_), channel_id=1, source_target_pairs={{0,64},{1,449},{64,128},{65,1},{128,192},{129,65},{192,256},{193,1... | collective-permute-start | bytes 393224 | tf_op jit(solution)/shard_map/ppermute | solution.py:371
  33.2 9.4 %collective-permute-start.6 = (bf16[64,8,128]{2,1,0:T(8,128)(2,1)}, bf16[64,8,128]{2,1,0:T(8,128)(2,1)}, u32[]{:S(2)}, u32[]{:S(2)}) collective-permute-start(bf16[64,8,128]{2,1,0:T(8,128)(2,1)} %slice.12.refs_0_), channel_id=1, source_target_pairs={{0,448},{1,65},{64,0},{65,129},{128,64},{129,193},{192,128},{193,2... | collective-permute-start | bytes 393224 | tf_op jit(solution)/shard_map/ppermute | solution.py:371
  36.6 9.8 %collective-permute-start.3 = (bf16[64,8,128]{2,1,0:T(8,128)(2,1)}, bf16[64,8,128]{2,1,0:T(8,128)(2,1)}, u32[]{:S(2)}, u32[]{:S(2)}) collective-permute-start(bf16[64,8,128]{2,1,0:T(8,128)(2,1)} %collective-permute-done.2.refs_1_), channel_id=1, source_target_pairs={{0,64},{1,449},{64,128},{65,1},{128,192},{129,65},{192,256},{193,1... | collective-permute-start | bytes 393224 | tf_op jit(solution)/shard_map/ppermute | solution.py:371
  42.5 12.5 %collective-permute-start.7 = (bf16[64,8,128]{2,1,0:T(8,128)(2,1)}, bf16[64,8,128]{2,1,0:T(8,128)(2,1)}, u32[]{:S(2)}, u32[]{:S(2)}) collective-permute-start(bf16[64,8,128]{2,1,0:T(8,128)(2,1)} %collective-permute-done.6.refs_7_), channel_id=1, source_target_pairs={{0,448},{1,65},{64,0},{65,129},{128,64},{129,193},{192,128},{193,2... | collective-permute-start | bytes 393224 | tf_op jit(solution)/shard_map/ppermute | solution.py:371
  46.4 10.5 %collective-permute-start.4 = (bf16[64,8,128]{2,1,0:T(8,128)(2,1)}, bf16[64,8,128]{2,1,0:T(8,128)(2,1)}, u32[]{:S(2)}, u32[]{:S(2)}) collective-permute-start(bf16[64,8,128]{2,1,0:T(8,128)(2,1)} %collective-permute-done.3.refs_2_), channel_id=1, source_target_pairs={{0,64},{1,449},{64,128},{65,1},{128,192},{129,65},{192,256},{193,1... | collective-permute-start | bytes 393224 | tf_op jit(solution)/shard_map/ppermute | solution.py:371
  55.0 9.0 %collective-permute-start.8 = (bf16[64,8,128]{2,1,0:T(8,128)(2,1)}, bf16[64,8,128]{2,1,0:T(8,128)(2,1)}, u32[]{:S(2)}, u32[]{:S(2)}) collective-permute-start(bf16[64,8,128]{2,1,0:T(8,128)(2,1)} %collective-permute-done.7.refs_6_), channel_id=1, source_target_pairs={{0,448},{1,65},{64,0},{65,129},{128,64},{129,193},{192,128},{193,2... | collective-permute-start | bytes 393224 | tf_op jit(solution)/shard_map/ppermute | solution.py:371
  56.9 10.9 %collective-permute-start.5 = (bf16[64,8,128]{2,1,0:T(8,128)(2,1)}, bf16[64,8,128]{2,1,0:T(8,128)(2,1)}, u32[]{:S(2)}, u32[]{:S(2)}) collective-permute-start(bf16[64,8,128]{2,1,0:T(8,128)(2,1)} %collective-permute-done.4.refs_3_), channel_id=1, source_target_pairs={{0,64},{1,449},{64,128},{65,1},{128,192},{129,65},{192,256},{193,1... | collective-permute-start | bytes 393224 | tf_op jit(solution)/shard_map/ppermute | solution.py:371
  73.7 12.2 %copy-start.4 = (s32[65536]{0:T(1024)S(1)}, s32[65536]{0:T(1024)}, u32[]{:S(2)}) copy-start(s32[65536]{0:T(1024)} %param.20) | copy-start | bytes 786436
  73.7 15.3 %copy-start.1 = (bf16[512,512]{1,0:T(8,128)(2,1)S(1)}, bf16[512,512]{1,0:T(8,128)(2,1)}, u32[]{:S(2)}) copy-start(bf16[512,512]{1,0:T(8,128)(2,1)} %wq_ref.1) | copy-start | bytes 1572868
  73.7 15.3 %copy-start.2 = (bf16[512,512]{1,0:T(8,128)(2,1)S(1)}, bf16[512,512]{1,0:T(8,128)(2,1)}, u32[]{:S(2)}) copy-start(bf16[512,512]{1,0:T(8,128)(2,1)} %wk_ref.3) | copy-start | bytes 1572868
  73.7 15.3 %copy-start.3 = (bf16[512,512]{1,0:T(8,128)(2,1)S(1)}, bf16[512,512]{1,0:T(8,128)(2,1)}, u32[]{:S(2)}) copy-start(bf16[512,512]{1,0:T(8,128)(2,1)} %wv_ref.3) | copy-start | bytes 1572868
  73.7 15.3 %copy-start.5 = (bf16[128,512]{1,0:T(8,128)(2,1)S(1)}, bf16[128,512]{1,0:T(8,128)(2,1)}, u32[]{:S(2)}) copy-start(bf16[128,512]{1,0:T(8,128)(2,1)} %x_ref.5) | copy-start | bytes 393220
  73.7 39.7 %all-to-all-start.2 = ((bf16[64,15,8,128]{3,2,1,0:T(8,128)(2,1)}), bf16[64,15,8,128]{3,2,1,0:T(8,128)(2,1)}, u32[]{:S(2)}, u32[]{:S(2)}) async-start(bf16[64,15,8,128]{3,2,1,0:T(8,128)(2,1)} %select.78), calls=%async_computation.2 | async-start | bytes 3932160 | tf_op jit(solution)/shard_map/all_to_all | solution.py:406
  86.2 27.3 %copy-start.7 = (bf16[512,512]{1,0:T(8,128)(2,1)S(1)}, bf16[512,512]{1,0:T(8,128)(2,1)}, u32[]{:S(2)}) copy-start(bf16[512,512]{1,0:T(8,128)(2,1)} %w_out_hbm.1) | copy-start | bytes 1572868
  86.2 27.3 %copy-start.9 = (f32[1024]{0:T(1024)S(1)}, f32[1024]{0:T(1024)}, u32[]{:S(2)}) copy-start(f32[1024]{0:T(1024)} %param.30) | copy-start | bytes 12292
  86.2 27.2 %copy-start.11 = (f32[512]{0:T(512)S(1)}, f32[512]{0:T(512)}, u32[]{:S(2)}) copy-start(f32[512]{0:T(512)} %param.27) | copy-start | bytes 6148
  86.2 27.2 %copy-start.13 = (f32[512]{0:T(512)S(1)}, f32[512]{0:T(512)}, u32[]{:S(2)}) copy-start(f32[512]{0:T(512)} %param.28) | copy-start | bytes 6148
  86.2 27.2 %copy-start.15 = (f32[512]{0:T(512)S(1)}, f32[512]{0:T(512)}, u32[]{:S(2)}) copy-start(f32[512]{0:T(512)} %param.32) | copy-start | bytes 6148
  86.3 27.2 %copy-start.17 = (f32[512]{0:T(512)S(1)}, f32[512]{0:T(512)}, u32[]{:S(2)}) copy-start(f32[512]{0:T(512)} %param.33) | copy-start | bytes 6148

commit v3 on v2

--- a/solution.py
+++ b/solution.py
@@ -167,11 +167,14 @@
         all_ref[at : at + source.shape[0]] = source[...]
         at += source.shape[0]
 
+    per_group = (list_ref.shape[0] - SLOTS) // SLAB_GROUPS
+
     def one(dest, carry):
         group, member = dest // MEMBERS, dest % MEMBERS
         at = start_ref[group, member] + jnp.minimum(at_ref[0], count_ref[group, member])
+        at = at + group * per_group
         for slot in range(SLOTS):
-            out_ref[dest, slot] = all_ref[list_ref[group, at + slot]]
+            out_ref[dest, slot] = all_ref[list_ref[at + slot]]
         return carry
 
     lax.fori_loop(0, SLAB_BLOCKS, one, 0, unroll=4)
@@ -352,7 +355,7 @@
     )
     place = jnp.sum(ahead.astype(jnp.int32), axis=-1)
     pairs = jnp.sum(jnp.where(place[:, None, :] == slot[None, :, None], key_slot[:, None, :], 0), axis=-1)
-    pairs = jnp.pad(pairs, ((0, 0), (0, SLOTS)))
+    pairs = jnp.concatenate([pairs.reshape(-1), jnp.zeros((SLOTS,), jnp.int32)])
     member = jnp.arange(MEMBERS, dtype=jnp.int32)[None, :, None]
     start = jnp.sum((query_index[:, None, :] < member).astype(jnp.int32), axis=-1)
     count = jnp.sum((query_index[:, None, :] == member).astype(jnp.int32), axis=-1)

time: 123 us -> 121 us (0.984); the launches traced: 122 us -> 118 us
  Pallas kernels: 18 us -> 14.1 us
    pallas_call x1, Pallas kernels: 8.39 us -> 5.99 us  [finish(): pl.pallas_call(finish_kernel, in_specs=[SMEM] + [VMEM] * 13 + [hbm] * 3,...]
    pallas_call x1, Pallas kernels: 5.87 us -> 4.35 us  [select(): pl.pallas_call(select_kernel, in_specs=[SMEM] * 4 + [VMEM] * len(gathered...]
where the time goes in v3:
time: 121 us; the launch traced here: 118 us
  starting transfers between devices  61.6 us (51%)
  waiting for transfers between devices  36.4 us (30%)
  Pallas kernels  14.1 us (12%)
  other arithmetic  2.5 us (2%)
  between operations  1.88 us (2%)
  local copies, waits for them, and re-layouts  1.65 us (1%)
    ppermute x7, starting transfers between devices, move(): return lax.ppermute(value, ('zhi', 'core'), pairs)  33 us
    all_to_all x2, waiting for transfers between devices, exchange(): return lax.all_to_all(value, SLAB, split_axis=0, concat_axis=0, tiled=True)  26.4 us
    all_to_all x2, starting transfers between devices, exchange(): return lax.all_to_all(value, SLAB, split_axis=0, concat_axis=0, tiled=True)  23 us
    ppermute x7, waiting for transfers between devices, move(): return lax.ppermute(value, ('zhi', 'core'), pairs)  9.97 us
    pallas_call x1, Pallas kernels, finish(): pl.pallas_call(finish_kernel, in_specs=[SMEM] + [VMEM] * 13 + [hbm] * 3,...  5.99 us
    ppermute x2, starting transfers between devices, swap(): lax.ppermute(x, AXES, [p for a, b in pairs for p in ((a, b), (b, a))])  5.61 us
    pallas_call x1, Pallas kernels, select(): pl.pallas_call(select_kernel, in_specs=[SMEM] * 4 + [VMEM] * len(gathered...  4.35 us
  transfers between devices with their start and end apart: 11, of which 7 were waited for; matrix products, arithmetic and copies ran while one was open for 3% of the time, Pallas kernels for 2%

profile of v3, /device:TPU:1, one launch (start us, length us, event | category | flops | bytes accessed | tf_op | source)
XLA Modules:
  0.0 118.4 jit_solution(6165731154669027055)
XLA Ops:
  0.0 1.6 %pack.1 = bf16[64,16,128]{2,1,0:T(8,128)(2,1)} custom-call(bf16[128,512]{1,0:T(8,128)(2,1)} %x_ref.5, s32[8,32]{1,0:T(8,128)} %bitcast.26, s32[1,32]{1,0:T(1,128)} %counts_ref.1), custom_call_target="tpu_custom_call" | custom-call | tf_op jit(solution)/shard_map/pack/pallas_call | solution.py:155
  1.6 10.9 %all-to-all-start.1 = ((bf16[64,16,128]{2,1,0:T(8,128)(2,1)}), bf16[64,16,128]{2,1,0:T(8,128)(2,1)S(1)}, u32[]{:S(2)}, u32[]{:S(2)}) async-start(bf16[64,16,128]{2,1,0:T(8,128)(2,1)} %pack.1), calls=%async_computation.1 | async-start | bytes 524288 | tf_op jit(solution)/shard_map/all_to_all | solution.py:409
  12.6 2.5 %collective-permute-start = (bf16[128,512]{1,0:T(8,128)(2,1)}, bf16[128,512]{1,0:T(8,128)(2,1)S(1)}, u32[]{:S(2)}, u32[]{:S(2)}) collective-permute-start(bf16[128,512]{1,0:T(8,128)(2,1)} %x_ref.5), channel_id=1, source_target_pairs={{0,1},{1,0},{2,3},{3,2},{4,5},{5,4},{6,7},{7,6},{8,9},{9,8},{10,11... | collective-permute-start | bytes 393224 | tf_op jit(solution)/shard_map/ppermute | solution.py:385
  15.1 3.1 %collective-permute-start.1 = (bf16[128,512]{1,0:T(8,128)(2,1)}, bf16[128,512]{1,0:T(8,128)(2,1)S(1)}, u32[]{:S(2)}, u32[]{:S(2)}) collective-permute-start(bf16[128,512]{1,0:T(8,128)(2,1)} %x_ref.5), channel_id=1, source_target_pairs={{1,2},{2,1},{3,4},{4,3},{5,6},{6,5},{7,8},{8,7},{9,10},{10,9},{11,... | collective-permute-start | bytes 393224 | tf_op jit(solution)/shard_map/ppermute | solution.py:385
  18.3 4.2 %all-to-all-done.1 = bf16[64,16,128]{2,1,0:T(8,128)(2,1)S(1)} async-done(((bf16[64,16,128]{2,1,0:T(8,128)(2,1)}), bf16[64,16,128]{2,1,0:T(8,128)(2,1)S(1)}, u32[]{:S(2)}, u32[]{:S(2)}) %all-to-all-start.1) | async-done | bytes 262176 | tf_op jit(solution)/shard_map/all_to_all | solution.py:409
  22.5 0.7 slice.12.refs_0_
  23.2 0.0 collective-permute-done.beside_ref
  23.2 0.0 collective-permute-done.1.across_ref
  23.2 10.0 %collective-permute-start.2 = (bf16[64,8,128]{2,1,0:T(8,128)(2,1)}, bf16[64,8,128]{2,1,0:T(8,128)(2,1)}, u32[]{:S(2)}, u32[]{:S(2)}) collective-permute-start(bf16[64,8,128]{2,1,0:T(8,128)(2,1)} %slice.12.refs_0_), channel_id=1, source_target_pairs={{0,64},{1,449},{64,128},{65,1},{128,192},{129,65},{192,256},{193,1... | collective-permute-start | bytes 393224 | tf_op jit(solution)/shard_map/ppermute | solution.py:374
  33.1 1.9 %collective-permute-start.6 = (bf16[64,8,128]{2,1,0:T(8,128)(2,1)}, bf16[64,8,128]{2,1,0:T(8,128)(2,1)}, u32[]{:S(2)}, u32[]{:S(2)}) collective-permute-start(bf16[64,8,128]{2,1,0:T(8,128)(2,1)} %slice.12.refs_0_), channel_id=1, source_target_pairs={{0,448},{1,65},{64,0},{65,129},{128,64},{129,193},{192,128},{193,2... | collective-permute-start | bytes 393224 | tf_op jit(solution)/shard_map/ppermute | solution.py:374
  35.1 0.1 reshape.189
  35.2 1.4 %collective-permute-done.2.refs_1_ = bf16[64,8,128]{2,1,0:T(8,128)(2,1)} collective-permute-done((bf16[64,8,128]{2,1,0:T(8,128)(2,1)}, bf16[64,8,128]{2,1,0:T(8,128)(2,1)}, u32[]{:S(2)}, u32[]{:S(2)}) %collective-permute-start.2) | collective-permute-done | bytes 131104 | tf_op jit(solution)/shard_map/ppermute | solution.py:374
  36.6 5.9 %collective-permute-start.3 = (bf16[64,8,128]{2,1,0:T(8,128)(2,1)}, bf16[64,8,128]{2,1,0:T(8,128)(2,1)}, u32[]{:S(2)}, u32[]{:S(2)}) collective-permute-start(bf16[64,8,128]{2,1,0:T(8,128)(2,1)} %collective-permute-done.2.refs_1_), channel_id=1, source_target_pairs={{0,64},{1,449},{64,128},{65,1},{128,192},{129,65},{192,256},{193,1... | collective-permute-start | bytes 393224 | tf_op jit(solution)/shard_map/ppermute | solution.py:374
  42.5 0.0 collective-permute-done.6.refs_7_
  42.5 1.9 %collective-permute-start.7 = (bf16[64,8,128]{2,1,0:T(8,128)(2,1)}, bf16[64,8,128]{2,1,0:T(8,128)(2,1)}, u32[]{:S(2)}, u32[]{:S(2)}) collective-permute-start(bf16[64,8,128]{2,1,0:T(8,128)(2,1)} %collective-permute-done.6.refs_7_), channel_id=1, source_target_pairs={{0,448},{1,65},{64,0},{65,129},{128,64},{129,193},{192,128},{193,2... | collective-permute-start | bytes 393224 | tf_op jit(solution)/shard_map/ppermute | solution.py:374
  44.4 1.9 %collective-permute-done.3.refs_2_ = bf16[64,8,128]{2,1,0:T(8,128)(2,1)} collective-permute-done((bf16[64,8,128]{2,1,0:T(8,128)(2,1)}, bf16[64,8,128]{2,1,0:T(8,128)(2,1)}, u32[]{:S(2)}, u32[]{:S(2)}) %collective-permute-start.3) | collective-permute-done | bytes 131104 | tf_op jit(solution)/shard_map/ppermute | solution.py:374
  46.4 5.9 %collective-permute-start.4 = (bf16[64,8,128]{2,1,0:T(8,128)(2,1)}, bf16[64,8,128]{2,1,0:T(8,128)(2,1)}, u32[]{:S(2)}, u32[]{:S(2)}) collective-permute-start(bf16[64,8,128]{2,1,0:T(8,128)(2,1)} %collective-permute-done.3.refs_2_), channel_id=1, source_target_pairs={{0,64},{1,449},{64,128},{65,1},{128,192},{129,65},{192,256},{193,1... | collective-permute-start | bytes 393224 | tf_op jit(solution)/shard_map/ppermute | solution.py:374
  52.3 0.5 convert_reduce_fusion
  52.8 2.2 %collective-permute-done.7.refs_6_ = bf16[64,8,128]{2,1,0:T(8,128)(2,1)} collective-permute-done((bf16[64,8,128]{2,1,0:T(8,128)(2,1)}, bf16[64,8,128]{2,1,0:T(8,128)(2,1)}, u32[]{:S(2)}, u32[]{:S(2)}) %collective-permute-start.7) | collective-permute-done | bytes 131104 | tf_op jit(solution)/shard_map/ppermute | solution.py:374
  55.0 1.9 %collective-permute-start.8 = (bf16[64,8,128]{2,1,0:T(8,128)(2,1)}, bf16[64,8,128]{2,1,0:T(8,128)(2,1)}, u32[]{:S(2)}, u32[]{:S(2)}) collective-permute-start(bf16[64,8,128]{2,1,0:T(8,128)(2,1)} %collective-permute-done.7.refs_6_), channel_id=1, source_target_pairs={{0,448},{1,65},{64,0},{65,129},{128,64},{129,193},{192,128},{193,2... | collective-permute-start | bytes 393224 | tf_op jit(solution)/shard_map/ppermute | solution.py:374
  56.9 0.0 collective-permute-done.4.refs_3_
  56.9 5.5 %collective-permute-start.5 = (bf16[64,8,128]{2,1,0:T(8,128)(2,1)}, bf16[64,8,128]{2,1,0:T(8,128)(2,1)}, u32[]{:S(2)}, u32[]{:S(2)}) collective-permute-start(bf16[64,8,128]{2,1,0:T(8,128)(2,1)} %collective-permute-done.4.refs_3_), channel_id=1, source_target_pairs={{0,64},{1,449},{64,128},{65,1},{128,192},{129,65},{192,256},{193,1... | collective-permute-start | bytes 393224 | tf_op jit(solution)/shard_map/ppermute | solution.py:374
  62.4 0.2 select_reduce_fusion
  62.6 0.7 convert_reduce_fusion.1
  63.4 0.6 collective-permute-done.8.refs_5_
  64.0 3.8 %collective-permute-done.5.refs_4_ = bf16[64,8,128]{2,1,0:T(8,128)(2,1)} collective-permute-done((bf16[64,8,128]{2,1,0:T(8,128)(2,1)}, bf16[64,8,128]{2,1,0:T(8,128)(2,1)}, u32[]{:S(2)}, u32[]{:S(2)}) %collective-permute-start.5) | collective-permute-done | bytes 131104 | tf_op jit(solution)/shard_map/ppermute | solution.py:374
  67.8 4.3 %select.78 = bf16[64,15,8,128]{3,2,1,0:T(8,128)(2,1)} custom-call(s32[1]{0:T(128)} %constant.125.clone.1.at_ref, s32[4,16]{1,0:T(4,128)} %get-tuple-element.343.start_ref, s32[4,16]{1,0:T(4,128)S(1)} %get-tuple-element.344.count_ref, s32[1039]{0:T(1024)S(1)} %concatenate.6.list_ref, bf16[64,8,128]{2,1,0:T(8,128)(2,1)} %slice.12.refs_0_, ...), custom_call_target="tpu_custom_call" | custom-call | bytes 8388608 | tf_op jit(solution)/shard_map/select/pallas_call | solution.py:184
  72.2 0.0 copy-start.3
  72.2 0.0 copy-start
  72.2 0.0 copy-start.1
  72.2 0.0 copy-start.2
  72.2 0.0 copy-start.4
  72.2 12.1 %all-to-all-start.2 = ((bf16[64,15,8,128]{3,2,1,0:T(8,128)(2,1)}), bf16[64,15,8,128]{3,2,1,0:T(8,128)(2,1)}, u32[]{:S(2)}, u32[]{:S(2)}) async-start(bf16[64,15,8,128]{3,2,1,0:T(8,128)(2,1)} %select.78), calls=%async_computation.2 | async-start | bytes 3932160 | tf_op jit(solution)/shard_map/all_to_all | solution.py:409
  84.3 0.0 copy-done.3
  84.3 0.1 fusion.8
  84.5 0.1 bitcast_select_fusion
  84.5 0.1 broadcast_in_dim.70.kid_ref
  84.7 0.0 copy-start.6
  84.7 0.0 copy-start.8
  84.7 0.0 copy-start.10
  84.7 0.0 copy-start.12
  84.7 0.0 copy-start.14
  84.7 0.0 copy-start.16
  84.7 0.1 fusion.3
  84.8 0.1 reshape.184
  84.9 0.6 dynamic_slice.11
  86.2 0.7 reduce_max.9
  87.6 0.0 copy-done
  87.6 0.0 copy-done.1
  87.6 0.0 copy-done.2
  87.6 0.0 copy-done.4
  87.6 2.1 %near.1 = (bf16[4,128,256]{2,1,0:T(8,128)(2,1)S(1)}, f32[4,256]{1,0:T(4,128)S(1)}, f32[4,256]{1,0:T(4,128)S(1)}, f32[512,128]{1,0:T(8,128)S(1)}) custom-call(bf16[128,512]{1,0:T(8,128)(2,1)S(1)} %collective-permute-done.beside_ref, bf16[128,512]{1,0:T(8,128)(2,1)S(1)} %copy-done.4, bf16[128,512]{1,0:T(8,128)(2,1)S(1)} %collective-permute-done.1.across_ref, ...), custom_call_target="tpu_custom_call" | custom-call | flops 1000000000 | bytes 3145728 | tf_op jit(solution)/shard_map/near/pallas_call | solution.py:134
  89.7 22.2 %all-to-all-done.2.held_ref = bf16[64,15,8,128]{3,2,1,0:T(8,128)(2,1)} async-done(((bf16[64,15,8,128]{3,2,1,0:T(8,128)(2,1)}), bf16[64,15,8,128]{3,2,1,0:T(8,128)(2,1)}, u32[]{:S(2)}, u32[]{:S(2)}) %all-to-all-start.2) | async-done | bytes 1966112 | tf_op jit(solution)/shard_map/all_to_all | solution.py:409
  111.9 0.0 copy-done.6
  111.9 0.0 copy-done.8
  111.9 0.0 copy-done.10
  111.9 0.0 copy-done.12
  112.0 0.0 copy-done.14
  112.0 0.0 copy-done.16
  112.0 6.0 %finish.3 = (f32[128,512]{1,0:T(8,128)}, f32[4,256]{1,0:T(4,128)S(1)}, f32[4,256]{1,0:T(4,128)}, f32[512,128]{1,0:T(8,128)S(1)}) custom-call(s32[1]{0:T(128)S(6)} %min.13.count_ref, bf16[64,15,8,128]{3,2,1,0:T(8,128)(2,1)} %all-to-all-done.2.held_ref, bf16[4,128,256]{2,1,0:T(8,128)(2,1)S(1)} %get-tuple-element.334.query_ref, bf16[512,512]{1,0:T(8,128)(2,1)S(1)} %copy-done.1, ...), custom_call_target="tpu_custom_call" | custom-call | flops 4000000000 | bytes 8388608 | tf_op jit(solution)/shard_map/finish/pallas_call | solution.py:311
  118.0 0.2 conditional.1
  (10 shorter events, 0.1 us)
Async XLA Ops:
  1.6 20.9 %all-to-all-start.1 = ((bf16[64,16,128]{2,1,0:T(8,128)(2,1)}), bf16[64,16,128]{2,1,0:T(8,128)(2,1)S(1)}, u32[]{:S(2)}, u32[]{:S(2)}) async-start(bf16[64,16,128]{2,1,0:T(8,128)(2,1)} %pack.1), calls=%async_computation.1 | async-start | bytes 524288 | tf_op jit(solution)/shard_map/all_to_all | solution.py:409
  12.6 10.6 %collective-permute-start = (bf16[128,512]{1,0:T(8,128)(2,1)}, bf16[128,512]{1,0:T(8,128)(2,1)S(1)}, u32[]{:S(2)}, u32[]{:S(2)}) collective-permute-start(bf16[128,512]{1,0:T(8,128)(2,1)} %x_ref.5), channel_id=1, source_target_pairs={{0,1},{1,0},{2,3},{3,2},{4,5},{5,4},{6,7},{7,6},{8,9},{9,8},{10,11... | collective-permute-start | bytes 393224 | tf_op jit(solution)/shard_map/ppermute | solution.py:385
  15.1 8.1 %collective-permute-start.1 = (bf16[128,512]{1,0:T(8,128)(2,1)}, bf16[128,512]{1,0:T(8,128)(2,1)S(1)}, u32[]{:S(2)}, u32[]{:S(2)}) collective-permute-start(bf16[128,512]{1,0:T(8,128)(2,1)} %x_ref.5), channel_id=1, source_target_pairs={{1,2},{2,1},{3,4},{4,3},{5,6},{6,5},{7,8},{8,7},{9,10},{10,9},{11,... | collective-permute-start | bytes 393224 | tf_op jit(solution)/shard_map/ppermute | solution.py:385
  23.2 13.4 %collective-permute-start.2 = (bf16[64,8,128]{2,1,0:T(8,128)(2,1)}, bf16[64,8,128]{2,1,0:T(8,128)(2,1)}, u32[]{:S(2)}, u32[]{:S(2)}) collective-permute-start(bf16[64,8,128]{2,1,0:T(8,128)(2,1)} %slice.12.refs_0_), channel_id=1, source_target_pairs={{0,64},{1,449},{64,128},{65,1},{128,192},{129,65},{192,256},{193,1... | collective-permute-start | bytes 393224 | tf_op jit(solution)/shard_map/ppermute | solution.py:374
  33.1 9.4 %collective-permute-start.6 = (bf16[64,8,128]{2,1,0:T(8,128)(2,1)}, bf16[64,8,128]{2,1,0:T(8,128)(2,1)}, u32[]{:S(2)}, u32[]{:S(2)}) collective-permute-start(bf16[64,8,128]{2,1,0:T(8,128)(2,1)} %slice.12.refs_0_), channel_id=1, source_target_pairs={{0,448},{1,65},{64,0},{65,129},{128,64},{129,193},{192,128},{193,2... | collective-permute-start | bytes 393224 | tf_op jit(solution)/shard_map/ppermute | solution.py:374
  36.6 9.8 %collective-permute-start.3 = (bf16[64,8,128]{2,1,0:T(8,128)(2,1)}, bf16[64,8,128]{2,1,0:T(8,128)(2,1)}, u32[]{:S(2)}, u32[]{:S(2)}) collective-permute-start(bf16[64,8,128]{2,1,0:T(8,128)(2,1)} %collective-permute-done.2.refs_1_), channel_id=1, source_target_pairs={{0,64},{1,449},{64,128},{65,1},{128,192},{129,65},{192,256},{193,1... | collective-permute-start | bytes 393224 | tf_op jit(solution)/shard_map/ppermute | solution.py:374
  42.5 12.5 %collective-permute-start.7 = (bf16[64,8,128]{2,1,0:T(8,128)(2,1)}, bf16[64,8,128]{2,1,0:T(8,128)(2,1)}, u32[]{:S(2)}, u32[]{:S(2)}) collective-permute-start(bf16[64,8,128]{2,1,0:T(8,128)(2,1)} %collective-permute-done.6.refs_7_), channel_id=1, source_target_pairs={{0,448},{1,65},{64,0},{65,129},{128,64},{129,193},{192,128},{193,2... | collective-permute-start | bytes 393224 | tf_op jit(solution)/shard_map/ppermute | solution.py:374
  46.4 10.5 %collective-permute-start.4 = (bf16[64,8,128]{2,1,0:T(8,128)(2,1)}, bf16[64,8,128]{2,1,0:T(8,128)(2,1)}, u32[]{:S(2)}, u32[]{:S(2)}) collective-permute-start(bf16[64,8,128]{2,1,0:T(8,128)(2,1)} %collective-permute-done.3.refs_2_), channel_id=1, source_target_pairs={{0,64},{1,449},{64,128},{65,1},{128,192},{129,65},{192,256},{193,1... | collective-permute-start | bytes 393224 | tf_op jit(solution)/shard_map/ppermute | solution.py:374
  55.0 9.0 %collective-permute-start.8 = (bf16[64,8,128]{2,1,0:T(8,128)(2,1)}, bf16[64,8,128]{2,1,0:T(8,128)(2,1)}, u32[]{:S(2)}, u32[]{:S(2)}) collective-permute-start(bf16[64,8,128]{2,1,0:T(8,128)(2,1)} %collective-permute-done.7.refs_6_), channel_id=1, source_target_pairs={{0,448},{1,65},{64,0},{65,129},{128,64},{129,193},{192,128},{193,2... | collective-permute-start | bytes 393224 | tf_op jit(solution)/shard_map/ppermute | solution.py:374
  56.9 10.9 %collective-permute-start.5 = (bf16[64,8,128]{2,1,0:T(8,128)(2,1)}, bf16[64,8,128]{2,1,0:T(8,128)(2,1)}, u32[]{:S(2)}, u32[]{:S(2)}) collective-permute-start(bf16[64,8,128]{2,1,0:T(8,128)(2,1)} %collective-permute-done.4.refs_3_), channel_id=1, source_target_pairs={{0,64},{1,449},{64,128},{65,1},{128,192},{129,65},{192,256},{193,1... | collective-permute-start | bytes 393224 | tf_op jit(solution)/shard_map/ppermute | solution.py:374
  72.2 12.2 %copy-start.3 = (s32[65536]{0:T(1024)S(1)}, s32[65536]{0:T(1024)}, u32[]{:S(2)}) copy-start(s32[65536]{0:T(1024)} %param.20) | copy-start | bytes 786436
  72.2 15.4 %copy-start = (bf16[512,512]{1,0:T(8,128)(2,1)S(1)}, bf16[512,512]{1,0:T(8,128)(2,1)}, u32[]{:S(2)}) copy-start(bf16[512,512]{1,0:T(8,128)(2,1)} %wq_ref.1) | copy-start | bytes 1572868
  72.2 15.4 %copy-start.1 = (bf16[512,512]{1,0:T(8,128)(2,1)S(1)}, bf16[512,512]{1,0:T(8,128)(2,1)}, u32[]{:S(2)}) copy-start(bf16[512,512]{1,0:T(8,128)(2,1)} %wk_ref.3) | copy-start | bytes 1572868
  72.2 15.4 %copy-start.2 = (bf16[512,512]{1,0:T(8,128)(2,1)S(1)}, bf16[512,512]{1,0:T(8,128)(2,1)}, u32[]{:S(2)}) copy-start(bf16[512,512]{1,0:T(8,128)(2,1)} %wv_ref.3) | copy-start | bytes 1572868
  72.2 15.4 %copy-start.4 = (bf16[128,512]{1,0:T(8,128)(2,1)S(1)}, bf16[128,512]{1,0:T(8,128)(2,1)}, u32[]{:S(2)}) copy-start(bf16[128,512]{1,0:T(8,128)(2,1)} %x_ref.5) | copy-start | bytes 393220
  72.2 39.7 %all-to-all-start.2 = ((bf16[64,15,8,128]{3,2,1,0:T(8,128)(2,1)}), bf16[64,15,8,128]{3,2,1,0:T(8,128)(2,1)}, u32[]{:S(2)}, u32[]{:S(2)}) async-start(bf16[64,15,8,128]{3,2,1,0:T(8,128)(2,1)} %select.78), calls=%async_computation.2 | async-start | bytes 3932160 | tf_op jit(solution)/shard_map/all_to_all | solution.py:409
  84.7 27.3 %copy-start.6 = (bf16[512,512]{1,0:T(8,128)(2,1)S(1)}, bf16[512,512]{1,0:T(8,128)(2,1)}, u32[]{:S(2)}) copy-start(bf16[512,512]{1,0:T(8,128)(2,1)} %w_out_hbm.1) | copy-start | bytes 1572868
  84.7 27.3 %copy-start.8 = (f32[1024]{0:T(1024)S(1)}, f32[1024]{0:T(1024)}, u32[]{:S(2)}) copy-start(f32[1024]{0:T(1024)} %param.30) | copy-start | bytes 12292
  84.7 27.2 %copy-start.10 = (f32[512]{0:T(512)S(1)}, f32[512]{0:T(512)}, u32[]{:S(2)}) copy-start(f32[512]{0:T(512)} %param.27) | copy-start | bytes 6148
  84.7 27.2 %copy-start.12 = (f32[512]{0:T(512)S(1)}, f32[512]{0:T(512)}, u32[]{:S(2)}) copy-start(f32[512]{0:T(512)} %param.28) | copy-start | bytes 6148
  84.7 27.2 %copy-start.14 = (f32[512]{0:T(512)S(1)}, f32[512]{0:T(512)}, u32[]{:S(2)}) copy-start(f32[512]{0:T(512)} %param.32) | copy-start | bytes 6148
  84.7 27.2 %copy-start.16 = (f32[512]{0:T(512)S(1)}, f32[512]{0:T(512)}, u32[]{:S(2)}) copy-start(f32[512]{0:T(512)} %param.33) | copy-start | bytes 6148
